TPU v7x, 32 devices: a whole 2x2x4 slice. The times are simulated.
32 devices in a mesh: beam: 2 (over x), freq: 16 (over z, y, core).
Axes of the slice: x: 2, y: 2, z: 4, core: 2. Of those that a mesh axis runs over, the one named last changes fastest.
Arguments:
- spectrum: bfloat16 [2, 65536], P(None, ('beam', 'freq')), parts along dimension 1, may hold values from -6 to 6
- template_bank: bfloat16 [2, 256, 1024], replicated, may hold values from -0.125 to 0.125
- template_index: int32 [128], replicated, may hold values from 0 to 255
Outputs:
- harmonic_sum: float32 [128, 65536], P(None, ('beam', 'freq')), parts along dimension 1
There are 2 independent parts, one for each index of `beam`. A program takes and returns all parts, laid end to end along the dimension named above; an argument that names none is the same for every part. Nothing has to cross between parts.
Inputs may be any that keep to these rules, and one draw needn't show every extreme that they name: `template_index`: entry z names the bank template of acceleration row z.
All inputs are finite; a program needn't handle non-finite values.
Results may differ from a plain program's by a relative error of at most 0.002.
Values may be sent and summed in bfloat16 or wider, within the bound.
No kernel may reach another device: no remote copies, remote signals or barrier semaphores. Data moves between devices by JAX's collectives and lax.ppermute only.
A program may use at most 64 MiB of HBM per device.

v0:
```python
import math

import jax
import jax.numpy as jnp
from jax import lax
from jax.sharding import PartitionSpec as P


def with_halo(cells, sides, width):
    for axis, dim in sides:
        count = lax.axis_size(axis)
        ends = count - 1
        head = lax.slice_in_dim(cells, 0, width, axis=dim)
        tail = lax.slice_in_dim(cells, cells.shape[dim] - width, cells.shape[dim], axis=dim)
        cells = jnp.concatenate(
            [
                lax.ppermute(tail, axis, [(i, (i + 1) % count) for i in range(ends)]),
                cells,
                lax.ppermute(head, axis, [((i + 1) % count, i) for i in range(ends)]),
            ],
            axis=dim,
        )
    return cells


def as_sent(array):

    def short(part):
        return part.astype(jnp.bfloat16) if part.dtype == jnp.float32 else part

    return jax.tree.map(short, array)


def correlate(window, template_re, template_im):
    row_count = template_re.shape[0]
    taps = template_re.shape[1]
    length = window.shape[1] - taps
    block = math.gcd(length, 512)
    block_count = length // block
    kernel = jnp.concatenate(
        [jnp.stack([template_re, -template_im], 1), jnp.stack([template_im, template_re], 1)], 0
    )

    def one_block(start):
        segment = lax.dynamic_slice_in_dim(window, start, block + taps, 1)
        correlated = lax.conv_general_dilated(
            segment[None],
            kernel,
            (1,),
            "VALID",
            dimension_numbers=("NCH", "OIH", "NCH"),
            preferred_element_type=jnp.float32,
        )[0]
        real_part = correlated[:row_count, :block]
        imag_part = correlated[row_count:, :block]
        return (real_part * real_part + imag_part * imag_part).astype(jnp.bfloat16)

    starts = jnp.arange(block_count, dtype=jnp.int32) * block
    powers = lax.map(one_block, starts)
    return jnp.transpose(powers, (1, 0, 2)).reshape(row_count, length)


def stretch(source, numerator, denominator):
    row_count, col_count = source.shape
    small_expand = (
        jnp.arange(denominator)[None, :] * numerator // denominator
        == jnp.arange(numerator)[:, None]
    ).astype(jnp.bfloat16)
    grouped = source.reshape(row_count // numerator, numerator, col_count)
    spread = jnp.einsum(
        "anc,nk->akc", grouped, small_expand, preferred_element_type=jnp.float32
    ).astype(jnp.bfloat16)
    new_rows = row_count // numerator * denominator
    group_cols = math.gcd(col_count // numerator, 128)
    block_expand = (
        jnp.arange(denominator * group_cols)[None, :] * numerator // denominator
        == jnp.arange(numerator * group_cols)[:, None]
    ).astype(jnp.bfloat16)
    blocks = spread.reshape(new_rows, col_count // (numerator * group_cols), numerator * group_cols)
    result = jnp.einsum("abn,nk->abk", blocks, block_expand, preferred_element_type=jnp.float32)
    return result.reshape(new_rows, col_count // numerator * denominator)


def tiles_out(columns_held, row_count, numerator, denominator, owners, device, tract_cols):
    span = owners * numerator // denominator
    targets = jnp.arange(owners, dtype=jnp.int32)
    offset = (device - targets * span) % owners
    valid = offset < span
    source_block = jnp.minimum((targets * span + offset) // owners, owners - 1)
    held = columns_held[:row_count].reshape(row_count, owners, tract_cols)
    picked = jnp.take(held, source_block, axis=1)
    picked = jnp.where(valid[None, :, None], picked, jnp.zeros_like(picked))
    return picked.reshape(row_count, owners * tract_cols)


def tiles_in(received, numerator, denominator, owners, device, tract_cols):
    row_count = received.shape[0]
    span = owners * numerator // denominator
    source_owner = (device * span + jnp.arange(span, dtype=jnp.int32)) % owners
    got = jnp.take(received.reshape(row_count, owners, tract_cols), source_owner, axis=1)
    return got.reshape(row_count, span * tract_cols)


def body(spectrum, template_bank, template_index):
    owners = lax.axis_size("freq")
    device = lax.axis_index("freq")
    taps = template_bank.shape[2]
    rows_all = template_index.shape[0]
    half_taps = taps // 2
    tract_cols = spectrum.shape[1] // owners
    one_hot = (
        template_index[:, None] == jnp.arange(template_bank.shape[1], dtype=jnp.int32)[None, :]
    ).astype(jnp.bfloat16)
    template_re = jnp.dot(one_hot, template_bank[0], preferred_element_type=jnp.float32).astype(
        jnp.bfloat16
    )
    template_im = jnp.dot(one_hot, template_bank[1], preferred_element_type=jnp.float32).astype(
        jnp.bfloat16
    )
    padded = with_halo(spectrum, (("freq", 1),), half_taps)
    plane = correlate(padded, template_re, template_im)
    held_rows = 3 * rows_all // 4
    columns_held = lax.all_to_all(
        as_sent(plane[:held_rows]), "freq", split_axis=1, concat_axis=1, tiled=True
    )
    total = plane.astype(jnp.float32)
    half_send = tiles_out(columns_held, rows_all // 2, 1, 2, owners, device, tract_cols)
    half_got = lax.all_to_all(
        as_sent(half_send), "freq", split_axis=1, concat_axis=1, tiled=True
    ).astype(half_send.dtype)
    total = total + stretch(tiles_in(half_got, 1, 2, owners, device, tract_cols), 1, 2)
    quarter_send = tiles_out(columns_held, rows_all // 4, 1, 4, owners, device, tract_cols)
    quarter_got = lax.all_to_all(
        as_sent(quarter_send), "freq", split_axis=1, concat_axis=1, tiled=True
    ).astype(quarter_send.dtype)
    total = total + stretch(tiles_in(quarter_got, 1, 4, owners, device, tract_cols), 1, 4)
    three_send = tiles_out(columns_held, held_rows, 3, 4, owners, device, tract_cols)
    three_got = lax.all_to_all(
        as_sent(three_send), "freq", split_axis=1, concat_axis=1, tiled=True
    ).astype(three_send.dtype)
    total = total + stretch(tiles_in(three_got, 3, 4, owners, device, tract_cols), 3, 4)
    return total


def solution(mesh):
    return jax.shard_map(
        body,
        mesh=mesh,
        in_specs=(P(None, ("beam", "freq")), P(), P()),
        out_specs=P(None, ("beam", "freq")),
        check_vma=False,
    )
```

profile of v0, /device:TPU:1, one launch (start us, length us, event | category | flops | bytes accessed | tf_op | source)
XLA Modules:
  0.0 281.2 jit_solution(6663480286862663322)
XLA Ops:
  0.0 0.7 fusion.67
  0.7 4.5 %collective-permute-start = (bf16[2,512]{1,0:T(2,128)(2,1)S(1)}, bf16[2,512]{1,0:T(2,128)(2,1)S(1)}, u32[]{:S(2)}, u32[]{:S(2)}) collective-permute-start(bf16[2,512]{1,0:T(2,128)(2,1)S(1)} %get-tuple-element.68), channel_id=1, source_target_pairs={{0,1},{1,2},{2,3},{3,4},{4,5},{5,6},{6,7},{7,8},{8,9},{9,10},{10,1... | collective-permute-start | bytes 6152 | tf_op jit(solution)/shard_map/ppermute | solution.py:17
  5.2 1.9 collective-permute-start.1
  8.7 0.6 compare_and_fusion.3
  9.8 0.6 compare_and_fusion.1
  10.4 0.6 fusion.62
  11.1 0.6 and_select_fusion.14
  11.7 0.6 compare_and_fusion.2
  12.8 0.6 compare_and_fusion.4
  13.4 0.6 add_select_fusion.1
  14.0 0.6 add_select_fusion
  14.6 1.3 convolution_convert_fusion.1
  16.0 1.3 fusion.5
  17.3 0.6 pad_clamp_fusion.5
  17.9 0.6 pad_clamp_fusion.1
  18.6 0.6 fusion.47
  19.2 0.9 copy.47
  20.2 195.0 %while.10 = (s32[]{:T(128)}, bf16[4,128,512]{1,2,0:T(8,128)(2,1)S(1)}, s32[4]{0:T(128)S(1)}, bf16[2,3072]{1,0:T(2,128)(2,1)S(1)}, bf16[256,2,1024]{0,1,2:T(2,128)(2,1)S(1)}, /*index=5*/s32[]{:T(128)}, s32[]{:T(128)}, s32[]{:T(128)}) while((s32[]{:T(128)}, bf16[4,128,512]{1,2,0:T(8,128)(2,1)S(1)}, s32[4]{0:T(128)S(1)}, ...), condition=%wide.region_1.2_spmd, body=%wide.region_0.1_spmd.sunk | while | flops 538181632 | bytes 3310739 | solution.py:59
  20.4 0.6 dynamic_slice.11
  23.0 0.6 copy.80
  23.7 38.6 %fusion.77 = f32[1,256,513]{1,0,2:T(1,128)S(1)} fusion(bf16[1,2,1536]{1,0,2:T(2,128)(2,1)S(1)} %copy.80, bf16[256,2,1024]{0,1,2:T(2,128)(2,1)S(1)} %get-tuple-element.127), kind=kOutput, calls=%fused_computation.215.clone.1 | convolution fusion | flops 537919488 | bytes 1580032 | tf_op jit(solution)/shard_map/while/body/eval_jaxpr/conv_general_dilated | solution.py:46
  68.4 0.6 dynamic_slice.11
  71.0 0.6 copy.80
  71.7 38.5 %fusion.77 = f32[1,256,513]{1,0,2:T(1,128)S(1)} fusion(bf16[1,2,1536]{1,0,2:T(2,128)(2,1)S(1)} %copy.80, bf16[256,2,1024]{0,1,2:T(2,128)(2,1)S(1)} %get-tuple-element.127), kind=kOutput, calls=%fused_computation.215.clone.1 | convolution fusion | flops 537919488 | bytes 1580032 | tf_op jit(solution)/shard_map/while/body/eval_jaxpr/conv_general_dilated | solution.py:46
  116.0 0.6 dynamic_slice.11
  118.6 0.6 copy.80
  119.2 38.5 %fusion.77 = f32[1,256,513]{1,0,2:T(1,128)S(1)} fusion(bf16[1,2,1536]{1,0,2:T(2,128)(2,1)S(1)} %copy.80, bf16[256,2,1024]{0,1,2:T(2,128)(2,1)S(1)} %get-tuple-element.127), kind=kOutput, calls=%fused_computation.215.clone.1 | convolution fusion | flops 537919488 | bytes 1580032 | tf_op jit(solution)/shard_map/while/body/eval_jaxpr/conv_general_dilated | solution.py:46
  163.8 0.6 dynamic_slice.11
  166.4 0.6 copy.80
  167.0 38.5 %fusion.77 = f32[1,256,513]{1,0,2:T(1,128)S(1)} fusion(bf16[1,2,1536]{1,0,2:T(2,128)(2,1)S(1)} %copy.80, bf16[256,2,1024]{0,1,2:T(2,128)(2,1)S(1)} %get-tuple-element.127), kind=kOutput, calls=%fused_computation.215.clone.1 | convolution fusion | flops 537919488 | bytes 1580032 | tf_op jit(solution)/shard_map/while/body/eval_jaxpr/conv_general_dilated | solution.py:46
  215.3 0.9 copy.49
  216.2 6.5 %all-to-all-start = ((bf16[96,16,128]{2,0,1:T(8,128)(2,1)}), bf16[96,16,128]{2,0,1:T(8,128)(2,1)S(1)}, u32[]{:S(2)}, u32[]{:S(2)}) async-start(bf16[96,16,128]{2,0,1:T(8,128)(2,1)} %copy.49), calls=%async_computation | async-start | bytes 786432 | tf_op jit(solution)/shard_map/all_to_all | solution.py:123
  222.9 11.7 %all-to-all-done = bf16[96,16,128]{2,0,1:T(8,128)(2,1)S(1)} async-done(((bf16[96,16,128]{2,0,1:T(8,128)(2,1)}), bf16[96,16,128]{2,0,1:T(8,128)(2,1)S(1)}, u32[]{:S(2)}, u32[]{:S(2)}) %all-to-all-start) | async-done | bytes 393248 | tf_op jit(solution)/shard_map/all_to_all | solution.py:123
  234.6 0.6 gather_fusion.2
  235.2 0.8 select_bitcast_fusion.2
  236.0 4.0 %all-to-all-start.2 = ((bf16[32,16,128]{2,0,1:T(8,128)(2,1)}), bf16[32,16,128]{2,0,1:T(8,128)(2,1)S(1)}, u32[]{:S(2)}, u32[]{:S(2)}) async-start(bf16[32,16,128]{2,0,1:T(8,128)(2,1)} %select_bitcast_fusion.2), calls=%async_computation.2 | async-start | bytes 262144 | tf_op jit(solution)/shard_map/all_to_all | solution.py:133
  239.9 0.7 gather_fusion
  240.7 0.7 gather_fusion.4
  241.5 0.8 select_bitcast_fusion.1
  242.3 4.5 %all-to-all-done.2 = bf16[32,16,128]{2,0,1:T(8,128)(2,1)S(1)} async-done(((bf16[32,16,128]{2,0,1:T(8,128)(2,1)}), bf16[32,16,128]{2,0,1:T(8,128)(2,1)S(1)}, u32[]{:S(2)}, u32[]{:S(2)}) %all-to-all-start.2) | async-done | bytes 131104 | tf_op jit(solution)/shard_map/all_to_all | solution.py:133
  246.8 4.5 %all-to-all-start.1 = ((bf16[64,16,128]{2,0,1:T(8,128)(2,1)}), bf16[64,16,128]{2,0,1:T(8,128)(2,1)S(1)}, u32[]{:S(2)}, u32[]{:S(2)}) async-start(bf16[64,16,128]{2,0,1:T(8,128)(2,1)} %select_bitcast_fusion.1), calls=%async_computation.1 | async-start | bytes 524288 | tf_op jit(solution)/shard_map/all_to_all | solution.py:128
  251.3 0.9 select_bitcast_fusion
  253.0 7.8 %all-to-all-done.1 = bf16[64,16,128]{2,0,1:T(8,128)(2,1)S(1)} async-done(((bf16[64,16,128]{2,0,1:T(8,128)(2,1)}), bf16[64,16,128]{2,0,1:T(8,128)(2,1)S(1)}, u32[]{:S(2)}, u32[]{:S(2)}) %all-to-all-start.1) | async-done | bytes 262176 | tf_op jit(solution)/shard_map/all_to_all | solution.py:128
  260.8 4.0 %all-to-all-start.3 = ((bf16[96,16,128]{2,0,1:T(8,128)(2,1)}), bf16[96,16,128]{2,0,1:T(8,128)(2,1)S(1)}, u32[]{:S(2)}, u32[]{:S(2)}) async-start(bf16[96,16,128]{2,0,1:T(8,128)(2,1)} %select_bitcast_fusion), calls=%async_computation.3 | async-start | bytes 786432 | tf_op jit(solution)/shard_map/all_to_all | solution.py:138
  265.2 0.6 gather_fusion.1
  266.7 10.1 %all-to-all-done.3 = bf16[96,16,128]{2,0,1:T(8,128)(2,1)S(1)} async-done(((bf16[96,16,128]{2,0,1:T(8,128)(2,1)}), bf16[96,16,128]{2,0,1:T(8,128)(2,1)S(1)}, u32[]{:S(2)}, u32[]{:S(2)}) %all-to-all-start.3) | async-done | bytes 393248 | tf_op jit(solution)/shard_map/all_to_all | solution.py:138
  276.8 0.6 gather_fusion.5
  279.7 1.3 copy.59
  (90 shorter events, 7.9 us)
Async XLA Ops:
  0.7 19.4 %collective-permute-start = (bf16[2,512]{1,0:T(2,128)(2,1)S(1)}, bf16[2,512]{1,0:T(2,128)(2,1)S(1)}, u32[]{:S(2)}, u32[]{:S(2)}) collective-permute-start(bf16[2,512]{1,0:T(2,128)(2,1)S(1)} %get-tuple-element.68), channel_id=1, source_target_pairs={{0,1},{1,2},{2,3},{3,4},{4,5},{5,6},{6,7},{7,8},{8,9},{9,10},{10,1... | collective-permute-start | bytes 6152 | tf_op jit(solution)/shard_map/ppermute | solution.py:17
  5.2 14.9 %collective-permute-start.1 = (bf16[2,512]{1,0:T(2,128)(2,1)S(1)}, bf16[2,512]{1,0:T(2,128)(2,1)S(1)}, u32[]{:S(2)}, u32[]{:S(2)}) collective-permute-start(bf16[2,512]{1,0:T(2,128)(2,1)S(1)} %get-tuple-element.69), channel_id=1, source_target_pairs={{1,0},{2,1},{3,2},{4,3},{5,4},{6,5},{7,6},{8,7},{9,8},{10,9},{11,1... | collective-permute-start | bytes 6152 | tf_op jit(solution)/shard_map/ppermute | solution.py:19
  19.2 1.0 copy-start.2
  215.2 20.0 %copy-start = (bf16[4,128,512]{1,2,0:T(8,128)(2,1)}, bf16[4,128,512]{1,2,0:T(8,128)(2,1)S(1)}, u32[]{:S(2)}) copy-start(bf16[4,128,512]{1,2,0:T(8,128)(2,1)S(1)} %get-tuple-element.32) | copy-start | bytes 1572868
  215.2 7.5 %copy-start.17 = (s32[16]{0:T(128)S(1)}, s32[16]{0:T(128)}, u32[]{:S(2)}) copy-start(s32[16]{0:T(128)} %fusion.62) | copy-start | bytes 196
  215.2 7.5 %copy-start.16 = (s32[12]{0:T(128)S(1)}, s32[12]{0:T(128)}, u32[]{:S(2)}) copy-start(s32[12]{0:T(128)} %fusion.65) | copy-start | bytes 148
  215.2 7.5 %copy-start.14 = (s32[4]{0:T(128)S(1)}, s32[4]{0:T(128)}, u32[]{:S(2)}) copy-start(s32[4]{0:T(128)} %fusion.63) | copy-start | bytes 52
  215.2 7.5 %copy-start.13 = (s32[8]{0:T(128)S(1)}, s32[8]{0:T(128)}, u32[]{:S(2)}) copy-start(s32[8]{0:T(128)} %fusion.61) | copy-start | bytes 100
  215.2 7.5 %copy-start.15 = (pred[12]{0:T(512)(128)(4,1)S(1)}, pred[12]{0:T(512)(128)(4,1)}, u32[]{:S(2)}) copy-start(pred[12]{0:T(512)(128)(4,1)} %compare_and_fusion.1) | copy-start | bytes 40
  215.3 19.9 %copy-start.11 = (pred[16]{0:T(512)(128)(4,1)S(1)}, pred[16]{0:T(512)(128)(4,1)}, u32[]{:S(2)}) copy-start(pred[16]{0:T(512)(128)(4,1)} %get-tuple-element.72) | copy-start | bytes 52
  215.3 19.9 %copy-start.12 = (pred[16]{0:T(512)(128)(4,1)S(1)}, pred[16]{0:T(512)(128)(4,1)}, u32[]{:S(2)}) copy-start(pred[16]{0:T(512)(128)(4,1)} %get-tuple-element.73) | copy-start | bytes 52
  216.2 18.4 %all-to-all-start = ((bf16[96,16,128]{2,0,1:T(8,128)(2,1)}), bf16[96,16,128]{2,0,1:T(8,128)(2,1)S(1)}, u32[]{:S(2)}, u32[]{:S(2)}) async-start(bf16[96,16,128]{2,0,1:T(8,128)(2,1)} %copy.49), calls=%async_computation | async-start | bytes 786432 | tf_op jit(solution)/shard_map/all_to_all | solution.py:123
  236.0 5.5 %copy-start.18 = (pred[16]{0:T(512)(128)(4,1)S(1)}, pred[16]{0:T(512)(128)(4,1)}, u32[]{:S(2)}) copy-start(pred[16]{0:T(512)(128)(4,1)} %get-tuple-element.74) | copy-start | bytes 52
  236.0 5.5 %copy-start.19 = (pred[16]{0:T(512)(128)(4,1)S(1)}, pred[16]{0:T(512)(128)(4,1)}, u32[]{:S(2)}) copy-start(pred[16]{0:T(512)(128)(4,1)} %get-tuple-element.75) | copy-start | bytes 52
  236.0 10.8 %all-to-all-start.2 = ((bf16[32,16,128]{2,0,1:T(8,128)(2,1)}), bf16[32,16,128]{2,0,1:T(8,128)(2,1)S(1)}, u32[]{:S(2)}, u32[]{:S(2)}) async-start(bf16[32,16,128]{2,0,1:T(8,128)(2,1)} %select_bitcast_fusion.2), calls=%async_computation.2 | async-start | bytes 262144 | tf_op jit(solution)/shard_map/all_to_all | solution.py:133
  240.7 10.6 %copy-start.8 = (pred[16]{0:T(512)(128)(4,1)S(1)}, pred[16]{0:T(512)(128)(4,1)}, u32[]{:S(2)}) copy-start(pred[16]{0:T(512)(128)(4,1)} %get-tuple-element.70) | copy-start | bytes 52
  240.7 10.6 %copy-start.9 = (pred[16]{0:T(512)(128)(4,1)S(1)}, pred[16]{0:T(512)(128)(4,1)}, u32[]{:S(2)}) copy-start(pred[16]{0:T(512)(128)(4,1)} %get-tuple-element.71) | copy-start | bytes 52
  241.4 11.3 %copy-start.7 = (pred[4]{0:T(512)(128)(4,1)S(1)}, pred[4]{0:T(512)(128)(4,1)}, u32[]{:S(2)}) copy-start(pred[4]{0:T(512)(128)(4,1)} %compare_and_fusion.3) | copy-start | bytes 16
  241.5 11.3 %copy-start.10 = (f32[4]{0:T(128)S(1)}, f32[4]{0:T(128)}, u32[]{:S(2)}) copy-start(f32[4]{0:T(128)} %fusion.47) | copy-start | bytes 52
  246.8 14.0 %all-to-all-start.1 = ((bf16[64,16,128]{2,0,1:T(8,128)(2,1)}), bf16[64,16,128]{2,0,1:T(8,128)(2,1)S(1)}, u32[]{:S(2)}, u32[]{:S(2)}) async-start(bf16[64,16,128]{2,0,1:T(8,128)(2,1)} %select_bitcast_fusion.1), calls=%async_computation.1 | async-start | bytes 524288 | tf_op jit(solution)/shard_map/all_to_all | solution.py:128
  251.3 13.6 %copy-start.4 = (s32[512]{0:T(512)S(1)}, s32[512]{0:T(512)}, u32[]{:S(2)}) copy-start(s32[512]{0:T(512)} %add_select_fusion.1) | copy-start | bytes 6148
  253.0 12.8 %copy-start.6 = (pred[8]{0:T(512)(128)(4,1)S(1)}, pred[8]{0:T(512)(128)(4,1)}, u32[]{:S(2)}) copy-start(pred[8]{0:T(512)(128)(4,1)} %compare_and_fusion.5) | copy-start | bytes 28
  260.8 16.0 %all-to-all-start.3 = ((bf16[96,16,128]{2,0,1:T(8,128)(2,1)}), bf16[96,16,128]{2,0,1:T(8,128)(2,1)S(1)}, u32[]{:S(2)}, u32[]{:S(2)}) async-start(bf16[96,16,128]{2,0,1:T(8,128)(2,1)} %select_bitcast_fusion), calls=%async_computation.3 | async-start | bytes 786432 | tf_op jit(solution)/shard_map/all_to_all | solution.py:138
  265.2 1.1 copy-start.5
  277.7 0.7 copy-start.3
  278.4 1.0 copy-start.1
where the time goes:
time: 284 us; the launch traced here: 281 us
  matrix products  158 us (56%)
  loops' own time  35 us (12%)
  waiting for transfers between devices  34.2 us (12%)
  starting transfers between devices  25.4 us (9%)
  local copies, waits for them, and re-layouts  14.8 us (5%)
  other arithmetic  12.8 us (5%)
    conv_general_dilated x4, matrix products, one_block(): lax.conv_general_dilated(segment[None], kernel, (1,), 'VALID', dimension_...  154 us
    another operation x1, loops' own time, correlate(): powers = lax.map(one_block, starts)  35 us
    all_to_all x1, waiting for transfers between devices, body(): lax.all_to_all(as_sent(plane[:held_rows]), 'freq', split_axis=1, concat_a...  11.7 us
    all_to_all x1, waiting for transfers between devices, body(): lax.all_to_all(as_sent(three_send), 'freq', split_axis=1, concat_axis=1,...  10.1 us
    all_to_all x1, waiting for transfers between devices, body(): lax.all_to_all(as_sent(half_send), 'freq', split_axis=1, concat_axis=1, t...  7.82 us
    all_to_all x1, starting transfers between devices, body(): lax.all_to_all(as_sent(plane[:held_rows]), 'freq', split_axis=1, concat_a...  6.45 us
  transfers between devices with their start and end apart: 6, of which 4 were waited for; matrix products, arithmetic and copies ran while one was open for 7% of the time, Pallas kernels for 0%

commit v1 on v0

v1 whole, which is shorter than its diff:
```python
import functools

import jax
import jax.numpy as jnp
from jax import lax
from jax.experimental import pallas as pl
from jax.experimental.pallas import tpu as pltpu
from jax.sharding import PartitionSpec as P

LANES = 128
HARMONICS = ((3, 4), (1, 2), (1, 4))
F32 = jnp.float32
BF16 = jnp.bfloat16


def iota(shape, dim):
    return lax.broadcasted_iota(jnp.int32, shape, dim)


def weights_kernel(index_ref, bank_ref, w_ref):
    rows = index_ref.shape[1]
    bank = bank_ref.shape[1]
    taps = bank_ref.shape[2]
    picked = (iota((bank, rows), 0) == index_ref[...]).astype(BF16)
    order = iota((LANES, LANES), 1)
    order = (order // 8) * 8 + 7 - order % 8
    flip = (iota((LANES, LANES), 0) == order).astype(BF16)
    for m in range(taps // LANES):
        part = []
        for c in range(2):
            chunk = bank_ref[c, :, m * LANES : (m + 1) * LANES]
            chunk = jnp.dot(chunk, flip, preferred_element_type=F32).astype(BF16)
            part.append(
                lax.dot_general(
                    picked, chunk, (((0,), (0,)), ((), ())), preferred_element_type=F32
                )
            )
        re, im = part
        w_ref[m, :rows, :LANES] = re.astype(BF16)
        w_ref[m, :rows, LANES:] = (-im).astype(BF16)
        w_ref[m, rows:, :LANES] = im.astype(BF16)
        w_ref[m, rows:, LANES:] = re.astype(BF16)


def hankel(window, h_ref):
    length = window.shape[1]
    kept = length - LANES
    for c in range(2):
        row = jnp.broadcast_to(window[c : c + 1, :], (8, length))
        for a in range(0, LANES // 8, 2):
            pair = [
                pltpu.roll(row, length - 8 * k - 7, 1, stride=1, stride_axis=0)[:, :kept]
                for k in (a, a + 1)
            ]
            at = c * LANES + 8 * a
            h_ref[at : at + 16, :kept] = jnp.concatenate(pair, 0).astype(BF16)


def power(w_ref, h_ref, rows, col, width):
    all_rows = w_ref.shape[1] // 2
    count = w_ref.shape[0]
    right = jnp.concatenate(
        [h_ref[:, col + m * LANES : col + m * LANES + width] for m in range(count)], 0
    )
    parts = []
    for start in (0, all_rows):
        left = jnp.concatenate([w_ref[m, start : start + rows, :] for m in range(count)], 1)
        parts.append(jnp.dot(left, right, preferred_element_type=F32))
    re, im = parts
    return (re * re + im * im).astype(BF16)


def plane_kernel(w_ref, all_ref, out_ref, line_ref, h_ref, own_ref, *planes):
    owners, _, block = all_ref.shape
    rows = out_ref.shape[0]
    taps = w_ref.shape[0] * LANES
    half = taps // 2
    device = lax.axis_index("freq")
    line_ref[:, :half] = jnp.zeros((2, half), F32)
    line_ref[:, half + owners * block :] = jnp.zeros((2, half), F32)
    for j in range(owners):
        line_ref[:, half + j * block : half + (j + 1) * block] = all_ref[j].astype(F32)
    tile = 256
    pieces = []
    for (num, den), plane_ref in zip(HARMONICS + ((1, 1),), planes + (own_ref,)):
        part_rows, part_cols = plane_ref.shape
        start = pl.multiple_of(device * part_cols, LANES)
        hankel(line_ref[:, pl.ds(start, part_cols + taps)], h_ref)
        for col in range(0, part_cols, tile):
            plane_ref[:, col : col + tile] = power(w_ref, h_ref, part_rows, col, tile)
        if den == 1:
            continue
        group = LANES * num
        wide = LANES * den
        groups = part_cols // group
        expand = (
            iota((group, wide), 1) * num // den == iota((group, wide), 0)
        ).astype(BF16)
        stacked = jnp.concatenate(
            [plane_ref[:, g * group : (g + 1) * group] for g in range(groups)], 0
        )
        spread = jnp.dot(stacked, expand, preferred_element_type=F32).astype(BF16)
        pieces.append(
            jnp.concatenate(
                [spread[g * part_rows : (g + 1) * part_rows] for g in range(groups)], 1
            )
        )
    picks = [
        (iota((rows, p.shape[0]), 0) * num // den == iota((rows, p.shape[0]), 1)).astype(BF16)
        for (num, den), p in zip(HARMONICS, pieces)
    ]
    total = jnp.dot(
        jnp.concatenate(picks, 1), jnp.concatenate(pieces, 0), preferred_element_type=F32
    )
    out_ref[...] = own_ref[...].astype(F32) + total


def body(spectrum, template_bank, template_index):
    owners = lax.axis_size("freq")
    block = spectrum.shape[1]
    rows = template_index.shape[0]
    taps = template_bank.shape[2]
    vmem = pl.BlockSpec(memory_space=pltpu.VMEM)
    weights = pl.pallas_call(
        weights_kernel,
        out_shape=jax.ShapeDtypeStruct((taps // LANES, 2 * rows, 2 * LANES), BF16),
        in_specs=[vmem] * 2,
        out_specs=vmem,
        compiler_params=pltpu.CompilerParams(vmem_limit_bytes=32 << 20),
    )(template_index.reshape(1, rows), template_bank)
    everything = lax.all_to_all(
        jnp.broadcast_to(spectrum, (owners, 2, block)), "freq", split_axis=0, concat_axis=0, tiled=True
    )
    return pl.pallas_call(
        plane_kernel,
        out_shape=jax.ShapeDtypeStruct((rows, block), F32),
        in_specs=[vmem] * 2,
        out_specs=vmem,
        scratch_shapes=[
            pltpu.VMEM((2, owners * block + taps), F32),
            pltpu.VMEM((2 * LANES, block + taps - LANES), BF16),
            pltpu.VMEM((rows, block), BF16),
        ]
        + [
            pltpu.VMEM((rows * num // den, block * num // den), BF16) for num, den in HARMONICS
        ],
        compiler_params=pltpu.CompilerParams(vmem_limit_bytes=48 << 20),
    )(weights, everything)


def solution(mesh):
    return jax.shard_map(
        body,
        mesh=mesh,
        in_specs=(P(None, ("beam", "freq")), P(), P()),
        out_specs=P(None, ("beam", "freq")),
        check_vma=False,
    )
```

time: 284 us -> 25.2 us (0.09)
  the two profiles are of different devices: /device:TPU:1 before, /device:TPU:0 now
where the time goes in v1:
time: 25.2 us; the launch traced here: 24.9 us
  Pallas kernels  8.98 us (36%)
  starting transfers between devices  7.39 us (29%)
  waiting for transfers between devices  5.21 us (21%)
  local copies, waits for them, and re-layouts  3.3 us (13%)
    pallas_call x1, Pallas kernels, body(): pl.pallas_call(plane_kernel, out_shape=jax.ShapeDtypeStruct((rows, block)...  8.14 us
    all_to_all x1, starting transfers between devices, body(): lax.all_to_all(jnp.broadcast_to(spectrum, (owners, 2, block)), 'freq', sp...  7.39 us
    all_to_all x1, waiting for transfers between devices, body(): lax.all_to_all(jnp.broadcast_to(spectrum, (owners, 2, block)), 'freq', sp...  5.21 us
    unnamed x4, local copies, waits for them, and re-layouts  1.87 us
    broadcast_in_dim x1, local copies, waits for them, and re-layouts, body(): jnp.broadcast_to(spectrum, (owners, 2, block))  1.42 us
    pallas_call x1, Pallas kernels, body(): pl.pallas_call(weights_kernel, out_shape=jax.ShapeDtypeStruct((taps // LA...  0.84 us
  transfers between devices with their start and end apart: 1, of which 1 were waited for; matrix products, arithmetic and copies ran while one was open for 0% of the time, Pallas kernels for 3%

profile of v1, /device:TPU:0, one launch (start us, length us, event | category | flops | bytes accessed | tf_op | source)
XLA Modules:
  0.0 24.9 jit_solution(14197500442215640425)
XLA Ops:
  0.0 1.4 %broadcast_in_dim.3 = bf16[16,2,2048]{2,1,0:T(2,128)(2,1)} broadcast(bf16[2,2048]{1,0:T(2,128)(2,1)} %param.3), dimensions={1,2} | broadcast | bytes 139264 | tf_op jit(solution)/shard_map/broadcast_in_dim | solution.py:132
  1.4 7.4 %all-to-all-start = ((bf16[16,2,2048]{2,1,0:T(2,128)(2,1)}), bf16[16,2,2048]{2,1,0:T(2,128)(2,1)S(1)}, u32[]{:S(2)}, u32[]{:S(2)}) async-start(bf16[16,2,2048]{2,1,0:T(2,128)(2,1)} %broadcast_in_dim.3), calls=%async_computation | async-start | bytes 262144 | tf_op jit(solution)/shard_map/all_to_all | solution.py:131
  8.8 0.0 copy-start.1
  8.8 0.6 %copy-done.1 = s32[128]{0:T(128)S(1)} copy-done((s32[128]{0:T(128)S(1)}, s32[128]{0:T(128)}, u32[]{:S(2)}) %copy-start.1) | copy-done | bytes 536
  9.5 0.0 copy-start
  9.5 1.2 %copy-done = bf16[2,256,1024]{2,1,0:T(8,128)(2,1)S(1)} copy-done((bf16[2,256,1024]{2,1,0:T(8,128)(2,1)S(1)}, bf16[2,256,1024]{2,1,0:T(8,128)(2,1)}, u32[]{:S(2)}) %copy-start) | copy-done | bytes 1048600
  10.7 0.8 %shard_map.37.w_ref = bf16[8,256,256]{2,1,0:T(8,128)(2,1)S(1)} custom-call(s32[1,128]{1,0:T(1,128)S(1)} %bitcast.1, bf16[2,256,1024]{2,1,0:T(8,128)(2,1)S(1)} %copy-done), custom_call_target="tpu_custom_call" | custom-call | tf_op jit(solution)/shard_map/pallas_call | solution.py:124
  11.5 5.2 %all-to-all-done.all_ref = bf16[16,2,2048]{2,1,0:T(2,128)(2,1)S(1)} async-done(((bf16[16,2,2048]{2,1,0:T(2,128)(2,1)}), bf16[16,2,2048]{2,1,0:T(2,128)(2,1)S(1)}, u32[]{:S(2)}, u32[]{:S(2)}) %all-to-all-start) | async-done | bytes 131104 | tf_op jit(solution)/shard_map/all_to_all | solution.py:131
  16.8 8.1 %shard_map.38 = f32[128,2048]{1,0:T(8,128)} custom-call(bf16[8,256,256]{2,1,0:T(8,128)(2,1)S(1)} %shard_map.37.w_ref, bf16[16,2,2048]{2,1,0:T(2,128)(2,1)S(1)} %all-to-all-done.all_ref), custom_call_target="tpu_custom_call" | custom-call | tf_op jit(solution)/shard_map/pallas_call | solution.py:134
Async XLA Ops:
  1.4 15.3 %all-to-all-start = ((bf16[16,2,2048]{2,1,0:T(2,128)(2,1)}), bf16[16,2,2048]{2,1,0:T(2,128)(2,1)S(1)}, u32[]{:S(2)}, u32[]{:S(2)}) async-start(bf16[16,2,2048]{2,1,0:T(2,128)(2,1)} %broadcast_in_dim.3), calls=%async_computation | async-start | bytes 262144 | tf_op jit(solution)/shard_map/all_to_all | solution.py:131
  8.8 0.7 %copy-start.1 = (s32[128]{0:T(128)S(1)}, s32[128]{0:T(128)}, u32[]{:S(2)}) copy-start(s32[128]{0:T(128)} %param.5) | copy-start | bytes 1540
  9.5 1.2 %copy-start = (bf16[2,256,1024]{2,1,0:T(8,128)(2,1)S(1)}, bf16[2,256,1024]{2,1,0:T(8,128)(2,1)}, u32[]{:S(2)}) copy-start(bf16[2,256,1024]{2,1,0:T(8,128)(2,1)} %bank_ref.1) | copy-start | bytes 3145732

commit v2 on v1

v2 whole, which is shorter than its diff:
```python
import jax
import jax.numpy as jnp
from jax import lax
from jax.experimental import pallas as pl
from jax.experimental.pallas import tpu as pltpu
from jax.sharding import PartitionSpec as P

LANES = 128
TILE = 256
HARMONICS = ((3, 4), (1, 2), (1, 4))
F32 = jnp.float32
BF16 = jnp.bfloat16
VMEM = pl.BlockSpec(memory_space=pltpu.VMEM)


def iota(shape, dim):
    return lax.broadcasted_iota(jnp.int32, shape, dim)


def dot(left, right):
    return jnp.dot(left, right, preferred_element_type=F32)


def square(pair):
    rows = pair.shape[0] // 2
    re, im = pair[:rows], pair[rows:]
    return (re * re + im * im).astype(BF16)


def hankel(window, h_ref):
    length = window.shape[1]
    kept = length - LANES
    for c in range(2):
        row = jnp.broadcast_to(window[c : c + 1, :], (8, length))
        for a in range(0, LANES // 8, 2):
            pair = [
                pltpu.roll(row, length - 8 * k - 7, 1, stride=1, stride_axis=0)[:, :kept]
                for k in (a, a + 1)
            ]
            at = c * LANES + 8 * a
            h_ref[at : at + 16, :kept] = jnp.concatenate(pair, 0).astype(BF16)


def hankel_tile(h_ref, col, steps, width=TILE):
    return jnp.concatenate(
        [h_ref[:, col + m * LANES : col + m * LANES + width] for m in steps], 0
    )


def weights(w_ref, steps, rows=None):
    all_rows = w_ref.shape[1] // 2
    if rows is None:
        return jnp.concatenate([w_ref[m] for m in steps], 1)
    return jnp.concatenate(
        [
            jnp.concatenate([w_ref[m, :rows], w_ref[m, all_rows : all_rows + rows]], 0)
            for m in steps
        ],
        1,
    )


def share_kernel(own_ref, shared_ref):
    for j in range(shared_ref.shape[0]):
        shared_ref[j] = own_ref[...]


def local_kernel(index_ref, bank_ref, own_ref, w_ref, inner_ref, edge_ref, h_ref):
    rows = index_ref.shape[1]
    bank = bank_ref.shape[1]
    taps = bank_ref.shape[2]
    half = taps // 2
    block = own_ref.shape[1]
    picked = (iota((bank, rows), 0) == index_ref[...]).astype(BF16)
    order = iota((LANES, LANES), 1)
    order = (order // 8) * 8 + 7 - order % 8
    flip = (iota((LANES, LANES), 0) == order).astype(BF16)
    count = taps // LANES
    for m in range(count):
        part = []
        for c in range(2):
            chunk = bank_ref[c, :, m * LANES : (m + 1) * LANES]
            chunk = dot(chunk, flip).astype(BF16)
            part.append(
                lax.dot_general(
                    picked, chunk, (((0,), (0,)), ((), ())), preferred_element_type=F32
                )
            )
        re, im = part
        w_ref[m, :rows, :LANES] = re.astype(BF16)
        w_ref[m, :rows, LANES:] = (-im).astype(BF16)
        w_ref[m, rows:, :LANES] = im.astype(BF16)
        w_ref[m, rows:, LANES:] = re.astype(BF16)
    zeros = jnp.zeros((2, half), F32)
    hankel(jnp.concatenate([zeros, own_ref[...].astype(F32), zeros], 1), h_ref)
    for col in range(0, block, TILE):
        steps = [
            m
            for m in range(count)
            if col + m * LANES + TILE + LANES - 1 > half and col + m * LANES < half + block
        ]
        got = dot(weights(w_ref, steps), hankel_tile(h_ref, col, steps))
        if half <= col < block - half:
            inner_ref[:, col - half : col - half + TILE] = square(got)
        else:
            at = col if col < half else col - block + 2 * half
            edge_ref[:, at : at + TILE] = got


def packed(w_ref, h_ref, rows, cols, pack):
    count = w_ref.shape[0]
    all_rows = w_ref.shape[1] // 2
    long = cols + (pack - 1) * LANES
    tiles = []
    left = jnp.concatenate(
        [
            jnp.concatenate(
                [w_ref[m + k, base : base + rows] for k in range(pack) for base in (0, all_rows)],
                0,
            )
            for m in range(0, count, pack)
        ],
        1,
    )
    col = 0
    while col < long:
        width = min(TILE, long - col)
        tiles.append(dot(left, hankel_tile(h_ref, col, range(0, count, pack), width)))
        col += width
    got = jnp.concatenate(tiles, 1)
    total = got[: 2 * rows, :cols]
    for k in range(1, pack):
        total = total + got[2 * rows * k : 2 * rows * (k + 1), k * LANES : k * LANES + cols]
    return square(total)


def plane_kernel(w_ref, inner_ref, edge_ref, all_ref, out_ref, line_ref, h_ref, side_ref, buffer_ref, sems):
    owners, _, block = all_ref.shape
    rows = w_ref.shape[1] // 2
    count = w_ref.shape[0]
    taps = count * LANES
    half = taps // 2
    device = lax.axis_index("freq")
    line_ref[:, :half] = jnp.zeros((2, half), F32)
    line_ref[:, half + owners * block :] = jnp.zeros((2, half), F32)
    for j in range(owners):
        line_ref[:, half + j * block : half + (j + 1) * block] = all_ref[j].astype(F32)

    pieces = []
    for num, den in HARMONICS:
        part_rows, part_cols = rows * num // den, block * num // den
        start = pl.multiple_of(device * part_cols, LANES)
        hankel(line_ref[:, pl.ds(start, part_cols + taps)], h_ref)
        pack = rows // part_rows
        if pack > 1:
            plane = packed(w_ref, h_ref, part_rows, part_cols, pack)
        else:
            left = weights(w_ref, range(count), part_rows)
            plane = jnp.concatenate(
                [
                    square(dot(left, hankel_tile(h_ref, col, range(count))))
                    for col in range(0, part_cols, TILE)
                ],
                1,
            )
        group = LANES * num
        wide = LANES * den
        groups = part_cols // group
        expand = (
            iota((group, wide), 1) * num // den == iota((group, wide), 0)
        ).astype(BF16)
        stacked = jnp.concatenate(
            [plane[:, g * group : (g + 1) * group] for g in range(groups)], 0
        )
        spread = dot(stacked, expand).astype(BF16)
        pieces.append(
            jnp.concatenate(
                [spread[g * part_rows : (g + 1) * part_rows] for g in range(groups)], 1
            )
        )

    own = pl.multiple_of(device * block, LANES)
    edges = []
    pad = jnp.zeros((2, 2 * LANES), F32)
    hankel(jnp.concatenate([line_ref[:, pl.ds(own, half)], pad], 1), side_ref)
    for col in range(0, half, TILE):
        steps = [m for m in range(count) if col + m * LANES < half]
        edges.append(edge_ref[:, col : col + TILE] + dot(weights(w_ref, steps), hankel_tile(side_ref, col, steps)))
    after = pl.multiple_of(own + half + block, LANES)
    hankel(jnp.concatenate([pad, line_ref[:, pl.ds(after, half)], pad[:, :LANES]], 1), side_ref)
    for col in range(0, half, TILE):
        steps = [m for m in range(count) if col + m * LANES >= 2 * half - 2 * LANES]
        shift = 2 * half - 2 * LANES
        edges.append(
            edge_ref[:, half + col : half + col + TILE]
            + dot(weights(w_ref, steps), hankel_tile(side_ref, col - shift, steps))
        )
    edges = [square(edge) for edge in edges]
    middle = len(edges) // 2
    own_plane = jnp.concatenate(edges[:middle] + [inner_ref[...]] + edges[middle:], 1)

    picks = jnp.concatenate(
        [
            (iota((rows, p.shape[0]), 0) * num // den == iota((rows, p.shape[0]), 1)).astype(BF16)
            for (num, den), p in zip(HARMONICS, pieces)
        ],
        1,
    )
    chunks = sems.shape[0]
    width = block // chunks
    copies = []
    for n in range(chunks):
        at = slice(n * width, (n + 1) * width)
        total = dot(picks, jnp.concatenate([p[:, at] for p in pieces], 0))
        buffer_ref[:, at] = own_plane[:, at].astype(F32) + total
        copy = pltpu.make_async_copy(buffer_ref.at[:, at], out_ref.at[:, at], sems.at[n])
        copy.start()
        copies.append(copy)
    for copy in copies:
        copy.wait()


def body(spectrum, template_bank, template_index):
    owners = lax.axis_size("freq")
    block = spectrum.shape[1]
    rows = template_index.shape[0]
    taps = template_bank.shape[2]
    half = taps // 2
    shared = pl.pallas_call(
        share_kernel,
        out_shape=jax.ShapeDtypeStruct((owners, 2, block), BF16),
        in_specs=[VMEM],
        out_specs=VMEM,
        name="share",
    )(spectrum)
    everything = lax.all_to_all(shared, "freq", split_axis=0, concat_axis=0, tiled=True)
    w, inner, edge = pl.pallas_call(
        local_kernel,
        out_shape=(
            jax.ShapeDtypeStruct((taps // LANES, 2 * rows, 2 * LANES), BF16),
            jax.ShapeDtypeStruct((rows, block - 2 * half), BF16),
            jax.ShapeDtypeStruct((2 * rows, 2 * half), F32),
        ),
        in_specs=[VMEM] * 3,
        out_specs=(VMEM,) * 3,
        scratch_shapes=[pltpu.VMEM((2 * LANES, block + taps - LANES), BF16)],
        compiler_params=pltpu.CompilerParams(vmem_limit_bytes=24 << 20),
        name="local",
    )(template_index.reshape(1, rows), template_bank, spectrum)
    return pl.pallas_call(
        plane_kernel,
        out_shape=jax.ShapeDtypeStruct((rows, block), F32),
        in_specs=[VMEM] * 4,
        out_specs=pl.BlockSpec(memory_space=pl.ANY),
        scratch_shapes=[
            pltpu.VMEM((2, owners * block + taps), F32),
            pltpu.VMEM((2 * LANES, block + taps - LANES), BF16),
            pltpu.VMEM((2 * LANES, half + LANES + TILE), BF16),
            pltpu.VMEM((rows, block), F32),
            pltpu.SemaphoreType.DMA((4,)),
        ],
        compiler_params=pltpu.CompilerParams(vmem_limit_bytes=32 << 20),
        name="plane",
    )(w, inner, edge, everything)


def solution(mesh):
    return jax.shard_map(
        body,
        mesh=mesh,
        in_specs=(P(None, ("beam", "freq")), P(), P()),
        out_specs=P(None, ("beam", "freq")),
        check_vma=False,
    )
```

time: 25.2 us -> 21.5 us (0.85)
  waiting for transfers between devices: 5.21 us -> 3.09 us
  local copies, waits for them, and re-layouts: 3.3 us -> 1.87 us
  Pallas kernels: 8.98 us -> 8.71 us
    pallas_call x1, Pallas kernels: 8.14 us -> 4.39 us  [body(): pl.pallas_call(plane_kernel, out_shape=jax.ShapeDtypeStruct((rows, block)...]
    pallas_call x1 -> x2, Pallas kernels: 0.84 us -> 4.32 us  [the longest x1 2.96 us: body(): pl.pallas_call(local_kernel, out_shape=(jax.ShapeDtypeStruct((taps // LAN...]
    all_to_all x1, waiting for transfers between devices: 5.21 us -> 3.09 us  [body(): lax.all_to_all(shared, 'freq', split_axis=0, concat_axis=0, tiled=True)]
    broadcast_in_dim x1 -> x0, local copies, waits for them, and re-layouts: 1.42 us -> none  [body(): jnp.broadcast_to(spectrum, (owners, 2, block))]
    unnamed x4 -> x6, local copies, waits for them, and re-layouts: 1.87 us -> 1.87 us
  transfers between devices with their start and end apart: 1 -> 1, of which waited for: 1 -> 1; matrix products, arithmetic and copies ran while one was open for 0% -> 0% of each run, Pallas kernels for 3% -> 14%
where the time goes in v2:
time: 21.5 us; the launch traced here: 21.2 us
  Pallas kernels  8.71 us (41%)
  starting transfers between devices  7.52 us (35%)
  waiting for transfers between devices  3.09 us (14%)
  local copies, waits for them, and re-layouts  1.87 us (9%)
    all_to_all x1, starting transfers between devices, body(): lax.all_to_all(shared, 'freq', split_axis=0, concat_axis=0, tiled=True)  7.52 us
    pallas_call x1, Pallas kernels, body(): pl.pallas_call(plane_kernel, out_shape=jax.ShapeDtypeStruct((rows, block)...  4.39 us
    all_to_all x1, waiting for transfers between devices, body(): lax.all_to_all(shared, 'freq', split_axis=0, concat_axis=0, tiled=True)  3.09 us
    pallas_call x1, Pallas kernels, body(): pl.pallas_call(local_kernel, out_shape=(jax.ShapeDtypeStruct((taps // LAN...  2.96 us
    unnamed x6, local copies, waits for them, and re-layouts  1.87 us
    pallas_call x1, Pallas kernels, body(): pl.pallas_call(share_kernel, out_shape=jax.ShapeDtypeStruct((owners, 2, b...  1.36 us
  transfers between devices with their start and end apart: 1, of which 1 were waited for; matrix products, arithmetic and copies ran while one was open for 0% of the time, Pallas kernels for 14%

profile of v2, /device:TPU:0, one launch (start us, length us, event | category | flops | bytes accessed | tf_op | source)
XLA Modules:
  0.0 21.2 jit_solution(3548331500456453075)
XLA Ops:
  0.0 1.4 %share.1 = bf16[16,2,2048]{2,1,0:T(2,128)(2,1)} custom-call(bf16[2,2048]{1,0:T(2,128)(2,1)} %own_ref.3), custom_call_target="tpu_custom_call" | custom-call | tf_op jit(solution)/shard_map/share/pallas_call | solution.py:229
  1.4 0.0 copy-start.1
  1.4 7.5 %all-to-all-start = ((bf16[16,2,2048]{2,1,0:T(2,128)(2,1)}), bf16[16,2,2048]{2,1,0:T(2,128)(2,1)S(1)}, u32[]{:S(2)}, u32[]{:S(2)}) async-start(bf16[16,2,2048]{2,1,0:T(2,128)(2,1)} %share.1), calls=%async_computation | async-start | bytes 262144 | tf_op jit(solution)/shard_map/all_to_all | solution.py:236
  8.9 0.0 copy-start.2
  8.9 0.0 copy-done.1
  8.9 0.6 %copy-done.2 = s32[128]{0:T(128)S(1)} copy-done((s32[128]{0:T(128)S(1)}, s32[128]{0:T(128)}, u32[]{:S(2)}) %copy-start.2) | copy-done | bytes 536
  9.5 0.0 copy-start
  9.5 1.2 %copy-done = bf16[2,256,1024]{2,1,0:T(8,128)(2,1)S(1)} copy-done((bf16[2,256,1024]{2,1,0:T(8,128)(2,1)S(1)}, bf16[2,256,1024]{2,1,0:T(8,128)(2,1)}, u32[]{:S(2)}) %copy-start) | copy-done | bytes 1048600
  10.8 3.0 %local.1 = (bf16[8,256,256]{2,1,0:T(8,128)(2,1)S(1)}, bf16[128,1024]{1,0:T(8,128)(2,1)S(1)}, f32[256,1024]{1,0:T(8,128)S(1)}) custom-call(s32[1,128]{1,0:T(1,128)S(1)} %bitcast.1, bf16[2,256,1024]{2,1,0:T(8,128)(2,1)S(1)} %copy-done, bf16[2,2048]{1,0:T(2,128)(2,1)S(1)} %copy-done.1), custom_call_target="tpu_custom_call" | custom-call | tf_op jit(solution)/shard_map/local/pallas_call | solution.py:237
  13.7 3.1 %all-to-all-done.all_ref = bf16[16,2,2048]{2,1,0:T(2,128)(2,1)S(1)} async-done(((bf16[16,2,2048]{2,1,0:T(2,128)(2,1)}), bf16[16,2,2048]{2,1,0:T(2,128)(2,1)S(1)}, u32[]{:S(2)}, u32[]{:S(2)}) %all-to-all-start) | async-done | bytes 131104 | tf_op jit(solution)/shard_map/all_to_all | solution.py:236
  16.8 4.4 %plane.1 = f32[128,2048]{1,0:T(8,128)} custom-call(bf16[8,256,256]{2,1,0:T(8,128)(2,1)S(1)} %get-tuple-element.8.w_ref, bf16[128,1024]{1,0:T(8,128)(2,1)S(1)} %get-tuple-element.9.inner_ref, f32[256,1024]{1,0:T(8,128)S(1)} %get-tuple-element.10.edge_ref, bf16[16,2,2048]{2,1,0:T(2,128)(2,1)S(1)} %all-to-all-done.all_ref), custom_call_target="tpu_custom_call" | custom-call | tf_op jit(solution)/shard_map/plane/pallas_call | solution.py:250
Async XLA Ops:
  1.4 7.5 %copy-start.1 = (bf16[2,2048]{1,0:T(2,128)(2,1)S(1)}, bf16[2,2048]{1,0:T(2,128)(2,1)}, u32[]{:S(2)}) copy-start(bf16[2,2048]{1,0:T(2,128)(2,1)} %own_ref.3) | copy-start | bytes 24580
  1.4 15.5 %all-to-all-start = ((bf16[16,2,2048]{2,1,0:T(2,128)(2,1)}), bf16[16,2,2048]{2,1,0:T(2,128)(2,1)S(1)}, u32[]{:S(2)}, u32[]{:S(2)}) async-start(bf16[16,2,2048]{2,1,0:T(2,128)(2,1)} %share.1), calls=%async_computation | async-start | bytes 262144 | tf_op jit(solution)/shard_map/all_to_all | solution.py:236
  8.9 0.7 %copy-start.2 = (s32[128]{0:T(128)S(1)}, s32[128]{0:T(128)}, u32[]{:S(2)}) copy-start(s32[128]{0:T(128)} %param.5) | copy-start | bytes 1540
  9.5 1.2 %copy-start = (bf16[2,256,1024]{2,1,0:T(8,128)(2,1)S(1)}, bf16[2,256,1024]{2,1,0:T(8,128)(2,1)}, u32[]{:S(2)}) copy-start(bf16[2,256,1024]{2,1,0:T(8,128)(2,1)} %bank_ref.1) | copy-start | bytes 3145732

commit v3 on v2

--- a/solution.py
+++ b/solution.py
@@ -11,6 +11,8 @@
 F32 = jnp.float32
 BF16 = jnp.bfloat16
 VMEM = pl.BlockSpec(memory_space=pltpu.VMEM)
+ANY = pl.BlockSpec(memory_space=pl.ANY)
+HBM = pl.BlockSpec(memory_space=pltpu.HBM)
 
 
 def iota(shape, dim):
@@ -65,17 +67,26 @@
         shared_ref[j] = own_ref[...]
 
 
-def local_kernel(index_ref, bank_ref, own_ref, w_ref, inner_ref, edge_ref, h_ref):
+def local_kernel(index_hbm, bank_hbm, own_hbm, w_ref, inner_ref, edge_ref, index_ref, bank_ref, own_ref, h_ref, sems):
     rows = index_ref.shape[1]
     bank = bank_ref.shape[1]
     taps = bank_ref.shape[2]
     half = taps // 2
     block = own_ref.shape[1]
-    picked = (iota((bank, rows), 0) == index_ref[...]).astype(BF16)
+    count = taps // LANES
+    arrays = ((own_hbm, own_ref), (index_hbm, index_ref), (bank_hbm, bank_ref))
+    copies = [pltpu.make_async_copy(*pair, sems.at[n]) for n, pair in enumerate(arrays)]
+    for copy in copies:
+        copy.start()
     order = iota((LANES, LANES), 1)
     order = (order // 8) * 8 + 7 - order % 8
     flip = (iota((LANES, LANES), 0) == order).astype(BF16)
-    count = taps // LANES
+    copies[0].wait()
+    zeros = jnp.zeros((2, half), F32)
+    hankel(jnp.concatenate([zeros, own_ref[...].astype(F32), zeros], 1), h_ref)
+    copies[1].wait()
+    picked = (iota((bank, rows), 0) == index_ref[...]).astype(BF16)
+    copies[2].wait()
     for m in range(count):
         part = []
         for c in range(2):
@@ -91,8 +102,6 @@
         w_ref[m, :rows, LANES:] = (-im).astype(BF16)
         w_ref[m, rows:, :LANES] = im.astype(BF16)
         w_ref[m, rows:, LANES:] = re.astype(BF16)
-    zeros = jnp.zeros((2, half), F32)
-    hankel(jnp.concatenate([zeros, own_ref[...].astype(F32), zeros], 1), h_ref)
     for col in range(0, block, TILE):
         steps = [
             m
@@ -134,20 +143,12 @@
     return square(total)
 
 
-def plane_kernel(w_ref, inner_ref, edge_ref, all_ref, out_ref, line_ref, h_ref, side_ref, buffer_ref, sems):
-    owners, _, block = all_ref.shape
+def write_pieces(w_ref, line_ref, h_refs, pieces_ref, device, block):
+    count = w_ref.shape[0]
     rows = w_ref.shape[1] // 2
-    count = w_ref.shape[0]
     taps = count * LANES
-    half = taps // 2
-    device = lax.axis_index("freq")
-    line_ref[:, :half] = jnp.zeros((2, half), F32)
-    line_ref[:, half + owners * block :] = jnp.zeros((2, half), F32)
-    for j in range(owners):
-        line_ref[:, half + j * block : half + (j + 1) * block] = all_ref[j].astype(F32)
-
-    pieces = []
-    for num, den in HARMONICS:
+    base = 0
+    for (num, den), h_ref in zip(HARMONICS, h_refs):
         part_rows, part_cols = rows * num // den, block * num // den
         start = pl.multiple_of(device * part_cols, LANES)
         hankel(line_ref[:, pl.ds(start, part_cols + taps)], h_ref)
@@ -173,27 +174,73 @@
             [plane[:, g * group : (g + 1) * group] for g in range(groups)], 0
         )
         spread = dot(stacked, expand).astype(BF16)
-        pieces.append(
-            jnp.concatenate(
-                [spread[g * part_rows : (g + 1) * part_rows] for g in range(groups)], 1
-            )
-        )
+        for g in range(groups):
+            pieces_ref[base : base + part_rows, g * wide : (g + 1) * wide] = spread[
+                g * part_rows : (g + 1) * part_rows
+            ]
+        base += part_rows
+
+
+def fill_line(line_ref, blocks_ref, half, blocks):
+    block = blocks_ref.shape[2]
+    end = half + blocks * block
+    line_ref[:, :half] = jnp.zeros((2, half), F32)
+    for j in range(blocks):
+        line_ref[:, half + j * block : half + (j + 1) * block] = blocks_ref[j].astype(F32)
+    line_ref[:, end : end + half] = jnp.zeros((2, half), F32)
+
+
+def pair_kernel(w_ref, own_ref, other_ref, pieces_ref, line_ref, *h_refs):
+    block = own_ref.shape[1]
+    half = w_ref.shape[0] * LANES // 2
+    device = lax.axis_index("freq")
+
+    @pl.when(device < 2)
+    def _():
+        line_ref[:, :half] = jnp.zeros((2, half), F32)
+        mine = pl.multiple_of(half + device * block, LANES)
+        theirs = pl.multiple_of(half + (1 - device) * block, LANES)
+        line_ref[:, pl.ds(mine, block)] = own_ref[...].astype(F32)
+        line_ref[:, pl.ds(theirs, block)] = other_ref[...].astype(F32)
+        write_pieces(w_ref, line_ref, h_refs, pieces_ref, device, block)
+
+
+def plane_kernel(
+    w_ref, inner_ref, edge_ref, early_ref, all_ref, out_ref, line_ref, side_ref, pieces_ref, buffer_ref, sems, *h_refs
+):
+    owners, _, block = all_ref.shape
+    rows = w_ref.shape[1] // 2
+    count = w_ref.shape[0]
+    half = count * LANES // 2
+    device = lax.axis_index("freq")
+    fill_line(line_ref, all_ref, half, owners)
+
+    @pl.when(device < 2)
+    def _():
+        pieces_ref[...] = early_ref[...]
+
+    @pl.when(device >= 2)
+    def _():
+        write_pieces(w_ref, line_ref, h_refs, pieces_ref, device, block)
 
     own = pl.multiple_of(device * block, LANES)
     edges = []
     pad = jnp.zeros((2, 2 * LANES), F32)
-    hankel(jnp.concatenate([line_ref[:, pl.ds(own, half)], pad], 1), side_ref)
+    hankel(jnp.concatenate([line_ref[:, pl.ds(own, half)], pad], 1), side_ref.at[0])
+    after = pl.multiple_of(own + half + block, LANES)
+    hankel(jnp.concatenate([pad, line_ref[:, pl.ds(after, half)], pad[:, :LANES]], 1), side_ref.at[1])
     for col in range(0, half, TILE):
         steps = [m for m in range(count) if col + m * LANES < half]
-        edges.append(edge_ref[:, col : col + TILE] + dot(weights(w_ref, steps), hankel_tile(side_ref, col, steps)))
-    after = pl.multiple_of(own + half + block, LANES)
-    hankel(jnp.concatenate([pad, line_ref[:, pl.ds(after, half)], pad[:, :LANES]], 1), side_ref)
+        edges.append(
+            edge_ref[:, col : col + TILE]
+            + dot(weights(w_ref, steps), hankel_tile(side_ref.at[0], col, steps))
+        )
+    shift = 2 * half - 2 * LANES
     for col in range(0, half, TILE):
-        steps = [m for m in range(count) if col + m * LANES >= 2 * half - 2 * LANES]
-        shift = 2 * half - 2 * LANES
+        steps = [m for m in range(count) if col + m * LANES >= shift]
         edges.append(
             edge_ref[:, half + col : half + col + TILE]
-            + dot(weights(w_ref, steps), hankel_tile(side_ref, col - shift, steps))
+            + dot(weights(w_ref, steps), hankel_tile(side_ref.at[1], col - shift, steps))
         )
     edges = [square(edge) for edge in edges]
     middle = len(edges) // 2
@@ -201,8 +248,11 @@
 
     picks = jnp.concatenate(
         [
-            (iota((rows, p.shape[0]), 0) * num // den == iota((rows, p.shape[0]), 1)).astype(BF16)
-            for (num, den), p in zip(HARMONICS, pieces)
+            (
+                iota((rows, rows * num // den), 0) * num // den
+                == iota((rows, rows * num // den), 1)
+            ).astype(BF16)
+            for num, den in HARMONICS
         ],
         1,
     )
@@ -211,8 +261,7 @@
     copies = []
     for n in range(chunks):
         at = slice(n * width, (n + 1) * width)
-        total = dot(picks, jnp.concatenate([p[:, at] for p in pieces], 0))
-        buffer_ref[:, at] = own_plane[:, at].astype(F32) + total
+        buffer_ref[:, at] = own_plane[:, at].astype(F32) + dot(picks, pieces_ref[:, at])
         copy = pltpu.make_async_copy(buffer_ref.at[:, at], out_ref.at[:, at], sems.at[n])
         copy.start()
         copies.append(copy)
@@ -226,14 +275,19 @@
     rows = template_index.shape[0]
     taps = template_bank.shape[2]
     half = taps // 2
+    all_pieces = sum(rows * num // den for num, den in HARMONICS)
+    hankels = [
+        pltpu.VMEM((2 * LANES, block * num // den + taps - LANES), BF16) for num, den in HARMONICS
+    ]
     shared = pl.pallas_call(
         share_kernel,
-        out_shape=jax.ShapeDtypeStruct((owners, 2, block), BF16),
+        out_shape=pltpu.VMEM((owners, 2, block), BF16),
         in_specs=[VMEM],
         out_specs=VMEM,
         name="share",
     )(spectrum)
     everything = lax.all_to_all(shared, "freq", split_axis=0, concat_axis=0, tiled=True)
+    other = lax.ppermute(spectrum, "freq", [(i, i ^ 1) for i in range(owners)])
     w, inner, edge = pl.pallas_call(
         local_kernel,
         out_shape=(
@@ -241,27 +295,43 @@
             jax.ShapeDtypeStruct((rows, block - 2 * half), BF16),
             jax.ShapeDtypeStruct((2 * rows, 2 * half), F32),
         ),
-        in_specs=[VMEM] * 3,
+        in_specs=[HBM] * 3,
         out_specs=(VMEM,) * 3,
-        scratch_shapes=[pltpu.VMEM((2 * LANES, block + taps - LANES), BF16)],
+        scratch_shapes=[
+            pltpu.VMEM((1, rows), jnp.int32),
+            pltpu.VMEM(template_bank.shape, BF16),
+            pltpu.VMEM(spectrum.shape, BF16),
+            pltpu.VMEM((2 * LANES, block + taps - LANES), BF16),
+            pltpu.SemaphoreType.DMA((3,)),
+        ],
         compiler_params=pltpu.CompilerParams(vmem_limit_bytes=24 << 20),
         name="local",
     )(template_index.reshape(1, rows), template_bank, spectrum)
+    early = pl.pallas_call(
+        pair_kernel,
+        out_shape=jax.ShapeDtypeStruct((all_pieces, block), BF16),
+        in_specs=[VMEM] * 3,
+        out_specs=VMEM,
+        scratch_shapes=[pltpu.VMEM((2, 2 * block + taps), F32)] + hankels,
+        compiler_params=pltpu.CompilerParams(vmem_limit_bytes=24 << 20),
+        name="pair",
+    )(w, spectrum, other)
     return pl.pallas_call(
         plane_kernel,
         out_shape=jax.ShapeDtypeStruct((rows, block), F32),
-        in_specs=[VMEM] * 4,
-        out_specs=pl.BlockSpec(memory_space=pl.ANY),
+        in_specs=[VMEM] * 5,
+        out_specs=ANY,
         scratch_shapes=[
             pltpu.VMEM((2, owners * block + taps), F32),
-            pltpu.VMEM((2 * LANES, block + taps - LANES), BF16),
-            pltpu.VMEM((2 * LANES, half + LANES + TILE), BF16),
+            pltpu.VMEM((2, 2 * LANES, half + TILE), BF16),
+            pltpu.VMEM((all_pieces, block), BF16),
             pltpu.VMEM((rows, block), F32),
             pltpu.SemaphoreType.DMA((4,)),
-        ],
+        ]
+        + hankels,
         compiler_params=pltpu.CompilerParams(vmem_limit_bytes=32 << 20),
         name="plane",
-    )(w, inner, edge, everything)
+    )(w, inner, edge, early, everything)
 
 
 def solution(mesh):

time: 21.5 us -> 19.2 us (0.89)
  the two profiles are of different devices: /device:TPU:0 before, /device:TPU:1 now
where the time goes in v3:
time: 19.2 us; the launch traced here: 18.8 us
  Pallas kernels  9.44 us (49%)
  starting transfers between devices  7.65 us (40%)
  local copies, waits for them, and re-layouts  1.71 us (9%)
    all_to_all x1, starting transfers between devices, body(): lax.all_to_all(shared, 'freq', split_axis=0, concat_axis=0, tiled=True)  7.48 us
    pallas_call x1, Pallas kernels, body(): pl.pallas_call(local_kernel, out_shape=(jax.ShapeDtypeStruct((taps // LAN...  3.37 us
    pallas_call x1, Pallas kernels, body(): pl.pallas_call(pair_kernel, out_shape=jax.ShapeDtypeStruct((all_pieces, b...  2.97 us
    pallas_call x1, Pallas kernels, body(): pl.pallas_call(plane_kernel, out_shape=jax.ShapeDtypeStruct((rows, block)...  1.74 us
    unnamed x6, local copies, waits for them, and re-layouts  1.71 us
    pallas_call x1, Pallas kernels, body(): pl.pallas_call(share_kernel, out_shape=pltpu.VMEM((owners, 2, block), BF1...  1.36 us
  transfers between devices with their start and end apart: 2, of which 0 were waited for; matrix products, arithmetic and copies ran while one was open for 0% of the time, Pallas kernels for 34%

profile of v3, /device:TPU:1, one launch (start us, length us, event | category | flops | bytes accessed | tf_op | source)
XLA Modules:
  0.0 18.8 jit_solution(8342141761551932446)
XLA Ops:
  0.0 1.4 %share.1 = bf16[16,2,2048]{2,1,0:T(2,128)(2,1)} custom-call(bf16[2,2048]{1,0:T(2,128)(2,1)} %own_ref.3), custom_call_target="tpu_custom_call" | custom-call | tf_op jit(solution)/shard_map/share/pallas_call | solution.py:282
  1.4 0.0 copy-start.1
  1.4 7.5 %all-to-all-start = ((bf16[16,2,2048]{2,1,0:T(2,128)(2,1)}), bf16[16,2,2048]{2,1,0:T(2,128)(2,1)S(1)}, u32[]{:S(2)}, u32[]{:S(2)}) async-start(bf16[16,2,2048]{2,1,0:T(2,128)(2,1)} %share.1), calls=%async_computation | async-start | bytes 262144 | tf_op jit(solution)/shard_map/all_to_all | solution.py:289
  8.8 0.0 copy-done.1
  8.8 0.0 copy-start.2
  8.9 0.2 collective-permute-start
  9.0 0.5 %copy-done.2 = s32[128]{0:T(128)S(1)} copy-done((s32[128]{0:T(128)S(1)}, s32[128]{0:T(128)}, u32[]{:S(2)}) %copy-start.2) | copy-done | bytes 536
  9.5 0.0 copy-start
  9.5 1.2 %copy-done = bf16[2,256,1024]{2,1,0:T(8,128)(2,1)S(1)} copy-done((bf16[2,256,1024]{2,1,0:T(8,128)(2,1)S(1)}, bf16[2,256,1024]{2,1,0:T(8,128)(2,1)}, u32[]{:S(2)}) %copy-start) | copy-done | bytes 1048600
  10.7 3.4 %local.1 = (bf16[8,256,256]{2,1,0:T(8,128)(2,1)S(1)}, bf16[128,1024]{1,0:T(8,128)(2,1)S(1)}, f32[256,1024]{1,0:T(8,128)S(1)}) custom-call(s32[1,128]{1,0:T(1,128)S(1)} %bitcast.1, bf16[2,256,1024]{2,1,0:T(8,128)(2,1)S(1)} %copy-done, bf16[2,2048]{1,0:T(2,128)(2,1)S(1)} %copy-done.1), custom_call_target="tpu_custom_call" | custom-call | tf_op jit(solution)/shard_map/local/pallas_call | solution.py:291
  14.1 0.0 collective-permute-done.other_ref
  14.1 3.0 %pair.1.early_ref = bf16[192,2048]{1,0:T(8,128)(2,1)S(1)} custom-call(bf16[8,256,256]{2,1,0:T(8,128)(2,1)S(1)} %get-tuple-element.8.w_ref, bf16[2,2048]{1,0:T(2,128)(2,1)S(1)} %copy-done.1, bf16[2,2048]{1,0:T(2,128)(2,1)S(1)} %collective-permute-done.other_ref), custom_call_target="tpu_custom_call" | custom-call | tf_op jit(solution)/shard_map/pair/pallas_call | solution.py:310
  17.1 0.0 all-to-all-done.all_ref
  17.1 1.7 %plane.1 = f32[128,2048]{1,0:T(8,128)} custom-call(bf16[8,256,256]{2,1,0:T(8,128)(2,1)S(1)} %get-tuple-element.8.w_ref, bf16[128,1024]{1,0:T(8,128)(2,1)S(1)} %get-tuple-element.9.inner_ref, f32[256,1024]{1,0:T(8,128)S(1)} %get-tuple-element.10.edge_ref, bf16[192,2048]{1,0:T(8,128)(2,1)S(1)} %pair.1.early_ref, bf16[16,2,2048]{2,1,0:T(2,128)(2,1)S(1)} %all-to-all-done.all_ref), custom_call_target="tpu_custom_call" | custom-call | tf_op jit(solution)/shard_map/plane/pallas_call | solution.py:319
Async XLA Ops:
  1.4 7.5 %copy-start.1 = (bf16[2,2048]{1,0:T(2,128)(2,1)S(1)}, bf16[2,2048]{1,0:T(2,128)(2,1)}, u32[]{:S(2)}) copy-start(bf16[2,2048]{1,0:T(2,128)(2,1)} %own_ref.3) | copy-start | bytes 24580
  1.4 15.7 %all-to-all-start = ((bf16[16,2,2048]{2,1,0:T(2,128)(2,1)}), bf16[16,2,2048]{2,1,0:T(2,128)(2,1)S(1)}, u32[]{:S(2)}, u32[]{:S(2)}) async-start(bf16[16,2,2048]{2,1,0:T(2,128)(2,1)} %share.1), calls=%async_computation | async-start | bytes 262144 | tf_op jit(solution)/shard_map/all_to_all | solution.py:289
  8.8 0.7 %copy-start.2 = (s32[128]{0:T(128)S(1)}, s32[128]{0:T(128)}, u32[]{:S(2)}) copy-start(s32[128]{0:T(128)} %param.5) | copy-start | bytes 1540
  8.9 5.3 %collective-permute-start = (bf16[2,2048]{1,0:T(2,128)(2,1)S(1)}, bf16[2,2048]{1,0:T(2,128)(2,1)S(1)}, u32[]{:S(2)}, u32[]{:S(2)}) collective-permute-start(bf16[2,2048]{1,0:T(2,128)(2,1)S(1)} %copy-done.1), channel_id=1, source_target_pairs={{0,1},{1,0},{2,3},{3,2},{4,5},{5,4},{6,7},{7,6},{8,9},{9,8},{10,11... | collective-permute-start | bytes 24584 | tf_op jit(solution)/shard_map/ppermute | solution.py:290
  9.5 1.2 %copy-start = (bf16[2,256,1024]{2,1,0:T(8,128)(2,1)S(1)}, bf16[2,256,1024]{2,1,0:T(8,128)(2,1)}, u32[]{:S(2)}) copy-start(bf16[2,256,1024]{2,1,0:T(8,128)(2,1)} %bank_hbm.1) | copy-start | bytes 3145732

commit v4 on v2

v4 whole, which is shorter than its diff:
```python
import jax
import jax.numpy as jnp
from jax import lax
from jax.experimental import pallas as pl
from jax.experimental.pallas import tpu as pltpu
from jax.sharding import PartitionSpec as P

LANES = 128
TILE = 256
HARMONICS = ((3, 4), (1, 2), (1, 4))
F32 = jnp.float32
BF16 = jnp.bfloat16
VMEM = pl.BlockSpec(memory_space=pltpu.VMEM)
ANY = pl.BlockSpec(memory_space=pl.ANY)


def iota(shape, dim):
    return lax.broadcasted_iota(jnp.int32, shape, dim)


def dot(left, right):
    return jnp.dot(left, right, preferred_element_type=F32)


def square(pair):
    rows = pair.shape[0] // 2
    re, im = pair[:rows], pair[rows:]
    return (re * re + im * im).astype(BF16)


def hankel(window, h_ref):
    length = window.shape[1]
    kept = length - LANES
    for c in range(2):
        row = jnp.broadcast_to(window[c : c + 1, :], (8, length))
        for a in range(0, LANES // 8, 2):
            pair = [
                pltpu.roll(row, length - 8 * k - 7, 1, stride=1, stride_axis=0)[:, :kept]
                for k in (a, a + 1)
            ]
            at = c * LANES + 8 * a
            h_ref[at : at + 16, :kept] = jnp.concatenate(pair, 0).astype(BF16)


def hankel_tile(h_ref, col, steps, width=TILE):
    return jnp.concatenate(
        [h_ref[:, col + m * LANES : col + m * LANES + width] for m in steps], 0
    )


def weights(w_ref, steps, rows=None):
    all_rows = w_ref.shape[1] // 2
    if rows is None:
        return jnp.concatenate([w_ref[m] for m in steps], 1)
    return jnp.concatenate(
        [
            jnp.concatenate([w_ref[m, :rows], w_ref[m, all_rows : all_rows + rows]], 0)
            for m in steps
        ],
        1,
    )


def first_kernel(mark_ref):
    mark_ref[...] = jnp.zeros(mark_ref.shape, F32)


def share_kernel(mark_ref, own_ref, index_ref, shared_ref, index_out_ref):
    for j in range(shared_ref.shape[0]):
        shared_ref[j] = own_ref[...]
    index_out_ref[...] = index_ref[...]


def local_kernel(index_ref, bank_ref, own_ref, w_ref, inner_ref, edge_ref, h_ref):
    rows = index_ref.shape[1]
    bank = bank_ref.shape[1]
    taps = bank_ref.shape[2]
    half = taps // 2
    block = own_ref.shape[1]
    count = taps // LANES
    order = iota((LANES, LANES), 1)
    order = (order // 8) * 8 + 7 - order % 8
    flip = (iota((LANES, LANES), 0) == order).astype(BF16)
    zeros = jnp.zeros((2, half), F32)
    hankel(jnp.concatenate([zeros, own_ref[...].astype(F32), zeros], 1), h_ref)
    picked = (iota((bank, rows), 0) == index_ref[...]).astype(BF16)
    for m in range(count):
        part = []
        for c in range(2):
            chunk = bank_ref[c, :, m * LANES : (m + 1) * LANES]
            chunk = dot(chunk, flip).astype(BF16)
            part.append(
                lax.dot_general(
                    picked, chunk, (((0,), (0,)), ((), ())), preferred_element_type=F32
                )
            )
        re, im = part
        w_ref[m, :rows, :LANES] = re.astype(BF16)
        w_ref[m, :rows, LANES:] = (-im).astype(BF16)
        w_ref[m, rows:, :LANES] = im.astype(BF16)
        w_ref[m, rows:, LANES:] = re.astype(BF16)
    for col in range(0, block, TILE):
        steps = [
            m
            for m in range(count)
            if col + m * LANES + TILE + LANES - 1 > half and col + m * LANES < half + block
        ]
        got = dot(weights(w_ref, steps), hankel_tile(h_ref, col, steps))
        if half <= col < block - half:
            inner_ref[:, col - half : col - half + TILE] = square(got)
        else:
            at = col if col < half else col - block + 2 * half
            edge_ref[:, at : at + TILE] = got


def packed(w_ref, h_ref, rows, cols, pack):
    count = w_ref.shape[0]
    all_rows = w_ref.shape[1] // 2
    long = cols + (pack - 1) * LANES
    tiles = []
    left = jnp.concatenate(
        [
            jnp.concatenate(
                [w_ref[m + k, base : base + rows] for k in range(pack) for base in (0, all_rows)],
                0,
            )
            for m in range(0, count, pack)
        ],
        1,
    )
    col = 0
    while col < long:
        width = min(TILE, long - col)
        tiles.append(dot(left, hankel_tile(h_ref, col, range(0, count, pack), width)))
        col += width
    got = jnp.concatenate(tiles, 1)
    total = got[: 2 * rows, :cols]
    for k in range(1, pack):
        total = total + got[2 * rows * k : 2 * rows * (k + 1), k * LANES : k * LANES + cols]
    return square(total)


def harmonic_plane(w_ref, line_ref, h_ref, device, num, den, block):
    count = w_ref.shape[0]
    rows = w_ref.shape[1] // 2
    part_rows, part_cols = rows * num // den, block * num // den
    start = pl.multiple_of(device * part_cols, LANES)
    hankel(line_ref[:, pl.ds(start, part_cols + count * LANES)], h_ref)
    pack = rows // part_rows
    if pack > 1:
        return packed(w_ref, h_ref, part_rows, part_cols, pack)
    left = weights(w_ref, range(count), part_rows)
    return jnp.concatenate(
        [
            square(dot(left, hankel_tile(h_ref, col, range(count))))
            for col in range(0, part_cols, TILE)
        ],
        1,
    )


def stretch(plane, num, den):
    part_rows, part_cols = plane.shape
    group = LANES * num
    wide = LANES * den
    groups = part_cols // group
    expand = (iota((group, wide), 1) * num // den == iota((group, wide), 0)).astype(BF16)
    stacked = jnp.concatenate([plane[:, g * group : (g + 1) * group] for g in range(groups)], 0)
    spread = dot(stacked, expand).astype(BF16)
    return jnp.concatenate([spread[g * part_rows : (g + 1) * part_rows] for g in range(groups)], 1)


def group_order(owners):
    first = owners * 3 // 4 - 1
    return (first, *(j for j in range(owners) if j != first))


def fill_line(line_ref, blocks_ref, half):
    owners, _, block = blocks_ref.shape
    end = half + owners * block
    line_ref[:, :half] = jnp.zeros((2, half), F32)
    for n, j in enumerate(group_order(owners)):
        line_ref[:, half + j * block : half + (j + 1) * block] = blocks_ref[n].astype(F32)
    line_ref[:, end : end + half] = jnp.zeros((2, half), F32)


def own_plane(w_ref, inner_ref, edge_ref, line_ref, side_ref, device, block):
    count = w_ref.shape[0]
    half = count * LANES // 2
    own = pl.multiple_of(device * block, LANES)
    edges = []
    pad = jnp.zeros((2, 2 * LANES), F32)
    hankel(jnp.concatenate([line_ref[:, pl.ds(own, half)], pad], 1), side_ref.at[0])
    after = pl.multiple_of(own + half + block, LANES)
    hankel(jnp.concatenate([pad, line_ref[:, pl.ds(after, half)], pad[:, :LANES]], 1), side_ref.at[1])
    for col in range(0, half, TILE):
        steps = [m for m in range(count) if col + m * LANES < half]
        edges.append(
            edge_ref[:, col : col + TILE]
            + dot(weights(w_ref, steps), hankel_tile(side_ref.at[0], col, steps))
        )
    shift = 2 * half - 2 * LANES
    for col in range(0, half, TILE):
        steps = [m for m in range(count) if col + m * LANES >= shift]
        edges.append(
            edge_ref[:, half + col : half + col + TILE]
            + dot(weights(w_ref, steps), hankel_tile(side_ref.at[1], col - shift, steps))
        )
    edges = [square(edge) for edge in edges]
    middle = len(edges) // 2
    return jnp.concatenate(edges[:middle] + [inner_ref[...]] + edges[middle:], 1)


def write_sum(own, pieces, out_ref, buffer_ref, sems):
    rows, block = buffer_ref.shape
    picks = jnp.concatenate(
        [
            (
                iota((rows, rows * num // den), 0) * num // den
                == iota((rows, rows * num // den), 1)
            ).astype(BF16)
            for num, den in HARMONICS
        ],
        1,
    )
    chunks = sems.shape[0]
    width = block // chunks
    copies = []
    for n in range(chunks):
        at = slice(n * width, (n + 1) * width)
        rest = dot(picks, jnp.concatenate([piece[:, at] for piece in pieces], 0))
        buffer_ref[:, at] = own[:, at].astype(F32) + rest
        copy = pltpu.make_async_copy(buffer_ref.at[:, at], out_ref.at[:, at], sems.at[n])
        copy.start()
        copies.append(copy)
    for copy in copies:
        copy.wait()


def plane_kernel(
    w_ref, inner_ref, edge_ref, all_ref, out_ref, line_ref, side_ref, buffer_ref, sems, *h_refs
):
    block = all_ref.shape[2]
    rows = w_ref.shape[1] // 2
    half = w_ref.shape[0] * LANES // 2
    device = lax.axis_index("freq")
    fill_line(line_ref, all_ref, half)

    @pl.when(device > 0)
    def _():
        pieces = [
            stretch(harmonic_plane(w_ref, line_ref, h_ref, device, num, den, block), num, den)
            for (num, den), h_ref in zip(HARMONICS, h_refs)
        ]
        own = own_plane(w_ref, inner_ref, edge_ref, line_ref, side_ref, device, block)
        write_sum(own, pieces, out_ref, buffer_ref, sems)

    @pl.when(device == 0)
    def _():
        own = own_plane(w_ref, inner_ref, edge_ref, line_ref, side_ref, 0, block)
        pieces = [
            stretch(own[: rows * num // den, : block * num // den], num, den)
            for num, den in HARMONICS
        ]
        write_sum(own, pieces, out_ref, buffer_ref, sems)


def body(spectrum, template_bank, template_index):
    owners = lax.axis_size("freq")
    block = spectrum.shape[1]
    rows = template_index.shape[0]
    taps = template_bank.shape[2]
    half = taps // 2
    hankels = [
        pltpu.VMEM((2 * LANES, block * num // den + taps - LANES), BF16) for num, den in HARMONICS
    ]
    mark = pl.pallas_call(
        first_kernel,
        out_shape=jax.ShapeDtypeStruct((8, LANES), F32),
        out_specs=VMEM,
        compiler_params=pltpu.CompilerParams(vmem_limit_bytes=1 << 20),
        cost_estimate=pl.CostEstimate(flops=4 * 10**9, bytes_accessed=16 << 20, transcendentals=0),
        name="first",
    )()
    shared, index = pl.pallas_call(
        share_kernel,
        out_shape=(
            jax.ShapeDtypeStruct((owners, 2, block), BF16),
            jax.ShapeDtypeStruct((1, rows), jnp.int32),
        ),
        in_specs=[ANY, VMEM, VMEM],
        out_specs=(VMEM,) * 2,
        compiler_params=pltpu.CompilerParams(vmem_limit_bytes=4 << 20),
        cost_estimate=pl.CostEstimate(flops=4 * 10**9, bytes_accessed=16 << 20, transcendentals=0),
        name="share",
    )(mark, spectrum, template_index.reshape(1, rows))
    everything = lax.all_to_all(
        shared,
        "freq",
        split_axis=0,
        concat_axis=0,
        tiled=True,
        axis_index_groups=[list(group_order(owners))],
    )
    w, inner, edge = pl.pallas_call(
        local_kernel,
        out_shape=(
            jax.ShapeDtypeStruct((taps // LANES, 2 * rows, 2 * LANES), BF16),
            jax.ShapeDtypeStruct((rows, block - 2 * half), BF16),
            jax.ShapeDtypeStruct((2 * rows, 2 * half), F32),
        ),
        in_specs=[VMEM] * 3,
        out_specs=(VMEM,) * 3,
        scratch_shapes=[pltpu.VMEM((2 * LANES, block + taps - LANES), BF16)],
        compiler_params=pltpu.CompilerParams(vmem_limit_bytes=24 << 20),
        name="local",
    )(index, template_bank, spectrum)
    return pl.pallas_call(
        plane_kernel,
        out_shape=jax.ShapeDtypeStruct((rows, block), F32),
        in_specs=[VMEM] * 4,
        out_specs=ANY,
        scratch_shapes=[
            pltpu.VMEM((2, owners * block + taps), F32),
            pltpu.VMEM((2, 2 * LANES, half + TILE), BF16),
            pltpu.VMEM((rows, block), F32),
            pltpu.SemaphoreType.DMA((4,)),
        ]
        + hankels,
        compiler_params=pltpu.CompilerParams(vmem_limit_bytes=32 << 20),
        name="plane",
    )(w, inner, edge, everything)


def solution(mesh):
    return jax.shard_map(
        body,
        mesh=mesh,
        in_specs=(P(None, ("beam", "freq")), P(), P()),
        out_specs=P(None, ("beam", "freq")),
        check_vma=False,
    )
```

time: 21.5 us -> 16.8 us (0.78)
  the two profiles are of different devices: /device:TPU:0 before, /device:TPU:1 now
where the time goes in v4:
time: 16.8 us; the launch traced here: 16.5 us
  Pallas kernels  7.97 us (47%)
  starting transfers between devices  7.43 us (44%)
  local copies, waits for them, and re-layouts  0.7 us (4%)
  waiting for transfers between devices  0.4 us (2%)
    all_to_all x1, starting transfers between devices, body(): lax.all_to_all(shared, 'freq', split_axis=0, concat_axis=0, tiled=True, a...  7.43 us
    pallas_call x1, Pallas kernels, body(): pl.pallas_call(plane_kernel, out_shape=jax.ShapeDtypeStruct((rows, block)...  4.36 us
    pallas_call x1, Pallas kernels, body(): pl.pallas_call(local_kernel, out_shape=(jax.ShapeDtypeStruct((taps // LAN...  2.94 us
    unnamed x6, local copies, waits for them, and re-layouts  0.7 us
    pallas_call x1, Pallas kernels, body(): pl.pallas_call(share_kernel, out_shape=(jax.ShapeDtypeStruct((owners, 2,...  0.66 us
    all_to_all x1, waiting for transfers between devices, body(): lax.all_to_all(shared, 'freq', split_axis=0, concat_axis=0, tiled=True, a...  0.4 us
  transfers between devices with their start and end apart: 1, of which 1 were waited for; matrix products, arithmetic and copies ran while one was open for 0% of the time, Pallas kernels for 18%

profile of v4, /device:TPU:1, one launch (start us, length us, event | category | flops | bytes accessed | tf_op | source)
XLA Modules:
  0.0 16.5 jit_solution(2750079561655698410)
XLA Ops:
  0.0 0.0 copy-start.1
  0.0 0.0 copy-start.2
  0.0 0.7 %copy-done.1 = bf16[2,2048]{1,0:T(2,128)(2,1)S(1)} copy-done((bf16[2,2048]{1,0:T(2,128)(2,1)S(1)}, bf16[2,2048]{1,0:T(2,128)(2,1)}, u32[]{:S(2)}) %copy-start.1) | copy-done | bytes 8216
  0.7 0.0 copy-done.2
  0.7 0.0 copy-start
  0.7 0.7 %share.1 = (bf16[16,2,2048]{2,1,0:T(2,128)(2,1)}, s32[1,128]{1,0:T(1,128)S(1)}) custom-call(f32[8,128]{1,0:T(8,128)S(1)} %first.1.mark_ref, bf16[2,2048]{1,0:T(2,128)(2,1)S(1)} %copy-done.1, s32[1,128]{1,0:T(1,128)S(1)} %bitcast.1), custom_call_target="tpu_custom_call" | custom-call | flops 4000000000 | bytes 16777216 | tf_op jit(solution)/shard_map/share/pallas_call | solution.py:285
  1.4 7.4 %all-to-all-start = ((bf16[16,2,2048]{2,1,0:T(2,128)(2,1)}), bf16[16,2,2048]{2,1,0:T(2,128)(2,1)S(1)}, u32[]{:S(2)}, u32[]{:S(2)}) async-start(bf16[16,2,2048]{2,1,0:T(2,128)(2,1)} %get-tuple-element.14), calls=%async_computation | async-start | bytes 262144 | tf_op jit(solution)/shard_map/all_to_all | solution.py:297
  8.8 0.0 copy-done
  8.8 2.9 %local.1 = (bf16[8,256,256]{2,1,0:T(8,128)(2,1)S(1)}, bf16[128,1024]{1,0:T(8,128)(2,1)S(1)}, f32[256,1024]{1,0:T(8,128)S(1)}) custom-call(s32[1,128]{1,0:T(1,128)S(1)} %get-tuple-element.10.index_ref, bf16[2,256,1024]{2,1,0:T(8,128)(2,1)S(1)} %copy-done, bf16[2,2048]{1,0:T(2,128)(2,1)S(1)} %copy-done.1), custom_call_target="tpu_custom_call" | custom-call | tf_op jit(solution)/shard_map/local/pallas_call | solution.py:305
  11.8 0.4 %all-to-all-done.all_ref = bf16[16,2,2048]{2,1,0:T(2,128)(2,1)S(1)} async-done(((bf16[16,2,2048]{2,1,0:T(2,128)(2,1)}), bf16[16,2,2048]{2,1,0:T(2,128)(2,1)S(1)}, u32[]{:S(2)}, u32[]{:S(2)}) %all-to-all-start) | async-done | bytes 131104 | tf_op jit(solution)/shard_map/all_to_all | solution.py:297
  12.2 4.4 %plane.1 = f32[128,2048]{1,0:T(8,128)} custom-call(bf16[8,256,256]{2,1,0:T(8,128)(2,1)S(1)} %get-tuple-element.11.w_ref, bf16[128,1024]{1,0:T(8,128)(2,1)S(1)} %get-tuple-element.12.inner_ref, f32[256,1024]{1,0:T(8,128)S(1)} %get-tuple-element.13.edge_ref, bf16[16,2,2048]{2,1,0:T(2,128)(2,1)S(1)} %all-to-all-done.all_ref), custom_call_target="tpu_custom_call" | custom-call | tf_op jit(solution)/shard_map/plane/pallas_call | solution.py:318
  (1 shorter events, 0.0 us)
Async XLA Ops:
  0.0 0.7 %copy-start.1 = (bf16[2,2048]{1,0:T(2,128)(2,1)S(1)}, bf16[2,2048]{1,0:T(2,128)(2,1)}, u32[]{:S(2)}) copy-start(bf16[2,2048]{1,0:T(2,128)(2,1)} %own_ref.3) | copy-start | bytes 24580
  0.0 0.7 %copy-start.2 = (s32[128]{0:T(128)S(1)}, s32[128]{0:T(128)}, u32[]{:S(2)}) copy-start(s32[128]{0:T(128)} %param.5) | copy-start | bytes 1540
  0.7 8.1 %copy-start = (bf16[2,256,1024]{2,1,0:T(8,128)(2,1)S(1)}, bf16[2,256,1024]{2,1,0:T(8,128)(2,1)}, u32[]{:S(2)}) copy-start(bf16[2,256,1024]{2,1,0:T(8,128)(2,1)} %bank_ref.1) | copy-start | bytes 3145732
  1.4 10.8 %all-to-all-start = ((bf16[16,2,2048]{2,1,0:T(2,128)(2,1)}), bf16[16,2,2048]{2,1,0:T(2,128)(2,1)S(1)}, u32[]{:S(2)}, u32[]{:S(2)}) async-start(bf16[16,2,2048]{2,1,0:T(2,128)(2,1)} %get-tuple-element.14), calls=%async_computation | async-start | bytes 262144 | tf_op jit(solution)/shard_map/all_to_all | solution.py:297

commit v5 on v4

--- a/solution.py
+++ b/solution.py
@@ -1,3 +1,5 @@
+import math
+
 import jax
 import jax.numpy as jnp
 from jax import lax
@@ -140,15 +142,16 @@
     return square(total)
 
 
-def harmonic_plane(w_ref, line_ref, h_ref, device, num, den, block):
+def harmonic_plane(w_ref, all_ref, h_ref, device, unit, num, den):
     count = w_ref.shape[0]
     rows = w_ref.shape[1] // 2
-    part_rows, part_cols = rows * num // den, block * num // den
-    start = pl.multiple_of(device * part_cols, LANES)
-    hankel(line_ref[:, pl.ds(start, part_cols + count * LANES)], h_ref)
+    taps = count * LANES
+    part_rows, part_cols = rows * num // den, all_ref.shape[2] * num // den
+    start = device * (part_cols // unit) - taps // 2 // unit
+    hankel(bins(all_ref, unit, start, (part_cols + taps) // unit), h_ref)
     pack = rows // part_rows
     if pack > 1:
-        return packed(w_ref, h_ref, part_rows, part_cols, pack)
+        return packed(w_ref, h_ref, part_rows, part_cols, min(pack, 2))
     left = weights(w_ref, range(count), part_rows)
     return jnp.concatenate(
         [
@@ -161,13 +164,21 @@
 
 def stretch(plane, num, den):
     part_rows, part_cols = plane.shape
-    group = LANES * num
-    wide = LANES * den
-    groups = part_cols // group
-    expand = (iota((group, wide), 1) * num // den == iota((group, wide), 0)).astype(BF16)
-    stacked = jnp.concatenate([plane[:, g * group : (g + 1) * group] for g in range(groups)], 0)
-    spread = dot(stacked, expand).astype(BF16)
-    return jnp.concatenate([spread[g * part_rows : (g + 1) * part_rows] for g in range(groups)], 1)
+    tiles = part_cols * den // num // TILE
+    starts = [j * TILE * num // den for j in range(tiles)]
+    wide = -(-(max(start % LANES for start in starts) + TILE * num // den) // LANES) * LANES
+    done = {}
+    for offset in sorted({start % LANES for start in starts}):
+        members = [j for j in range(tiles) if starts[j] % LANES == offset]
+        expand = (
+            iota((wide, TILE), 1) * num // den + offset == iota((wide, TILE), 0)
+        ).astype(BF16)
+        bases = [starts[j] - offset for j in members]
+        stacked = jnp.concatenate([plane[:, base : base + wide] for base in bases], 0)
+        spread = dot(stacked, expand).astype(BF16)
+        for n, j in enumerate(members):
+            done[j] = spread[n * part_rows : (n + 1) * part_rows]
+    return jnp.concatenate([done[j] for j in range(tiles)], 1)
 
 
 def group_order(owners):
@@ -175,24 +186,34 @@
     return (first, *(j for j in range(owners) if j != first))
 
 
-def fill_line(line_ref, blocks_ref, half):
-    owners, _, block = blocks_ref.shape
-    end = half + owners * block
-    line_ref[:, :half] = jnp.zeros((2, half), F32)
-    for n, j in enumerate(group_order(owners)):
-        line_ref[:, half + j * block : half + (j + 1) * block] = blocks_ref[n].astype(F32)
-    line_ref[:, end : end + half] = jnp.zeros((2, half), F32)
-
-
-def own_plane(w_ref, inner_ref, edge_ref, line_ref, side_ref, device, block):
+def bins(all_ref, unit, start, count):
+    owners, _, block = all_ref.shape
+    per = block // unit
+    first = group_order(owners)[0]
+    got = []
+    for k in range(count):
+        at = start + k
+        inside = jnp.logical_and(at >= 0, at < owners * per)
+        at = jnp.clip(at, 0, owners * per - 1)
+        owner = at // per
+        slot = jnp.where(owner == first, 0, jnp.where(owner < first, owner + 1, owner))
+        column = pl.multiple_of((at - owner * per) * unit, LANES)
+        piece = all_ref[slot, :, pl.ds(column, unit)].astype(F32)
+        got.append(jnp.where(inside, piece, 0.0))
+    return jnp.concatenate(got, 1)
+
+
+def own_plane(w_ref, inner_ref, edge_ref, all_ref, side_ref, device, unit):
     count = w_ref.shape[0]
     half = count * LANES // 2
-    own = pl.multiple_of(device * block, LANES)
+    width = half // unit
+    here = device * (all_ref.shape[2] // unit)
     edges = []
     pad = jnp.zeros((2, 2 * LANES), F32)
-    hankel(jnp.concatenate([line_ref[:, pl.ds(own, half)], pad], 1), side_ref.at[0])
-    after = pl.multiple_of(own + half + block, LANES)
-    hankel(jnp.concatenate([pad, line_ref[:, pl.ds(after, half)], pad[:, :LANES]], 1), side_ref.at[1])
+    before = bins(all_ref, unit, here - width, width)
+    hankel(jnp.concatenate([before, pad], 1), side_ref.at[0])
+    after = bins(all_ref, unit, here + all_ref.shape[2] // unit, width)
+    hankel(jnp.concatenate([pad, after, pad[:, :LANES]], 1), side_ref.at[1])
     for col in range(0, half, TILE):
         steps = [m for m in range(count) if col + m * LANES < half]
         edges.append(
@@ -238,26 +259,27 @@
 
 
 def plane_kernel(
-    w_ref, inner_ref, edge_ref, all_ref, out_ref, line_ref, side_ref, buffer_ref, sems, *h_refs
+    w_ref, inner_ref, edge_ref, all_ref, out_ref, side_ref, buffer_ref, sems, *h_refs
 ):
     block = all_ref.shape[2]
     rows = w_ref.shape[1] // 2
     half = w_ref.shape[0] * LANES // 2
     device = lax.axis_index("freq")
-    fill_line(line_ref, all_ref, half)
+    unit = math.gcd(half, *(block * num // den for num, den in HARMONICS))
 
     @pl.when(device > 0)
     def _():
-        pieces = [
-            stretch(harmonic_plane(w_ref, line_ref, h_ref, device, num, den, block), num, den)
+        planes = [
+            harmonic_plane(w_ref, all_ref, h_ref, device, unit, num, den)
             for (num, den), h_ref in zip(HARMONICS, h_refs)
         ]
-        own = own_plane(w_ref, inner_ref, edge_ref, line_ref, side_ref, device, block)
+        pieces = [stretch(plane, num, den) for plane, (num, den) in zip(planes, HARMONICS)]
+        own = own_plane(w_ref, inner_ref, edge_ref, all_ref, side_ref, device, unit)
         write_sum(own, pieces, out_ref, buffer_ref, sems)
 
     @pl.when(device == 0)
     def _():
-        own = own_plane(w_ref, inner_ref, edge_ref, line_ref, side_ref, 0, block)
+        own = own_plane(w_ref, inner_ref, edge_ref, all_ref, side_ref, device, unit)
         pieces = [
             stretch(own[: rows * num // den, : block * num // den], num, den)
             for num, den in HARMONICS
@@ -321,7 +343,6 @@
         in_specs=[VMEM] * 4,
         out_specs=ANY,
         scratch_shapes=[
-            pltpu.VMEM((2, owners * block + taps), F32),
             pltpu.VMEM((2, 2 * LANES, half + TILE), BF16),
             pltpu.VMEM((rows, block), F32),
             pltpu.SemaphoreType.DMA((4,)),

time: 16.8 us -> 16.6 us (0.988)
  Pallas kernels: 7.97 us -> 7.76 us
    pallas_call x1, Pallas kernels: 4.36 us -> 4.15 us  [body(): pl.pallas_call(plane_kernel, out_shape=jax.ShapeDtypeStruct((rows, block)...]
where the time goes in v5:
time: 16.6 us; the launch traced here: 16.3 us
  Pallas kernels  7.76 us (47%)
  starting transfers between devices  7.43 us (45%)
  local copies, waits for them, and re-layouts  0.7 us (4%)
  waiting for transfers between devices  0.4 us (2%)
    all_to_all x1, starting transfers between devices, body(): lax.all_to_all(shared, 'freq', split_axis=0, concat_axis=0, tiled=True, a...  7.43 us
    pallas_call x1, Pallas kernels, body(): pl.pallas_call(plane_kernel, out_shape=jax.ShapeDtypeStruct((rows, block)...  4.15 us
    pallas_call x1, Pallas kernels, body(): pl.pallas_call(local_kernel, out_shape=(jax.ShapeDtypeStruct((taps // LAN...  2.94 us
    unnamed x6, local copies, waits for them, and re-layouts  0.7 us
    pallas_call x1, Pallas kernels, body(): pl.pallas_call(share_kernel, out_shape=(jax.ShapeDtypeStruct((owners, 2,...  0.66 us
    all_to_all x1, waiting for transfers between devices, body(): lax.all_to_all(shared, 'freq', split_axis=0, concat_axis=0, tiled=True, a...  0.4 us
  transfers between devices with their start and end apart: 1, of which 1 were waited for; matrix products, arithmetic and copies ran while one was open for 0% of the time, Pallas kernels for 18%

profile of v5, /device:TPU:1, one launch (start us, length us, event | category | flops | bytes accessed | tf_op | source)
XLA Modules:
  0.0 16.3 jit_solution(6141652757981111375)
XLA Ops:
  0.0 0.0 copy-start.1
  0.0 0.0 copy-start.2
  0.0 0.7 %copy-done.1 = bf16[2,2048]{1,0:T(2,128)(2,1)S(1)} copy-done((bf16[2,2048]{1,0:T(2,128)(2,1)S(1)}, bf16[2,2048]{1,0:T(2,128)(2,1)}, u32[]{:S(2)}) %copy-start.1) | copy-done | bytes 8216
  0.7 0.0 copy-done.2
  0.7 0.0 copy-start
  0.7 0.7 %share.1 = (bf16[16,2,2048]{2,1,0:T(2,128)(2,1)}, s32[1,128]{1,0:T(1,128)S(1)}) custom-call(f32[8,128]{1,0:T(8,128)S(1)} %first.1.mark_ref, bf16[2,2048]{1,0:T(2,128)(2,1)S(1)} %copy-done.1, s32[1,128]{1,0:T(1,128)S(1)} %bitcast.1), custom_call_target="tpu_custom_call" | custom-call | flops 4000000000 | bytes 16777216 | tf_op jit(solution)/shard_map/share/pallas_call | solution.py:307
  1.4 7.4 %all-to-all-start = ((bf16[16,2,2048]{2,1,0:T(2,128)(2,1)}), bf16[16,2,2048]{2,1,0:T(2,128)(2,1)S(1)}, u32[]{:S(2)}, u32[]{:S(2)}) async-start(bf16[16,2,2048]{2,1,0:T(2,128)(2,1)} %get-tuple-element.14), calls=%async_computation | async-start | bytes 262144 | tf_op jit(solution)/shard_map/all_to_all | solution.py:319
  8.8 0.0 copy-done
  8.8 2.9 %local.1 = (bf16[8,256,256]{2,1,0:T(8,128)(2,1)S(1)}, bf16[128,1024]{1,0:T(8,128)(2,1)S(1)}, f32[256,1024]{1,0:T(8,128)S(1)}) custom-call(s32[1,128]{1,0:T(1,128)S(1)} %get-tuple-element.10.index_ref, bf16[2,256,1024]{2,1,0:T(8,128)(2,1)S(1)} %copy-done, bf16[2,2048]{1,0:T(2,128)(2,1)S(1)} %copy-done.1), custom_call_target="tpu_custom_call" | custom-call | tf_op jit(solution)/shard_map/local/pallas_call | solution.py:327
  11.8 0.4 %all-to-all-done.all_ref = bf16[16,2,2048]{2,1,0:T(2,128)(2,1)S(1)} async-done(((bf16[16,2,2048]{2,1,0:T(2,128)(2,1)}), bf16[16,2,2048]{2,1,0:T(2,128)(2,1)S(1)}, u32[]{:S(2)}, u32[]{:S(2)}) %all-to-all-start) | async-done | bytes 131104 | tf_op jit(solution)/shard_map/all_to_all | solution.py:319
  12.2 4.1 %plane.1 = f32[128,2048]{1,0:T(8,128)} custom-call(bf16[8,256,256]{2,1,0:T(8,128)(2,1)S(1)} %get-tuple-element.11.w_ref, bf16[128,1024]{1,0:T(8,128)(2,1)S(1)} %get-tuple-element.12.inner_ref, f32[256,1024]{1,0:T(8,128)S(1)} %get-tuple-element.13.edge_ref, bf16[16,2,2048]{2,1,0:T(2,128)(2,1)S(1)} %all-to-all-done.all_ref), custom_call_target="tpu_custom_call" | custom-call | tf_op jit(solution)/shard_map/plane/pallas_call | solution.py:340
  (1 shorter events, 0.0 us)
Async XLA Ops:
  0.0 0.7 %copy-start.1 = (bf16[2,2048]{1,0:T(2,128)(2,1)S(1)}, bf16[2,2048]{1,0:T(2,128)(2,1)}, u32[]{:S(2)}) copy-start(bf16[2,2048]{1,0:T(2,128)(2,1)} %own_ref.3) | copy-start | bytes 24580
  0.0 0.7 %copy-start.2 = (s32[128]{0:T(128)S(1)}, s32[128]{0:T(128)}, u32[]{:S(2)}) copy-start(s32[128]{0:T(128)} %param.5) | copy-start | bytes 1540
  0.7 8.1 %copy-start = (bf16[2,256,1024]{2,1,0:T(8,128)(2,1)S(1)}, bf16[2,256,1024]{2,1,0:T(8,128)(2,1)}, u32[]{:S(2)}) copy-start(bf16[2,256,1024]{2,1,0:T(8,128)(2,1)} %bank_ref.1) | copy-start | bytes 3145732
  1.4 10.8 %all-to-all-start = ((bf16[16,2,2048]{2,1,0:T(2,128)(2,1)}), bf16[16,2,2048]{2,1,0:T(2,128)(2,1)S(1)}, u32[]{:S(2)}, u32[]{:S(2)}) async-start(bf16[16,2,2048]{2,1,0:T(2,128)(2,1)} %get-tuple-element.14), calls=%async_computation | async-start | bytes 262144 | tf_op jit(solution)/shard_map/all_to_all | solution.py:319

commit v6 on v5

--- a/solution.py
+++ b/solution.py
@@ -118,28 +118,31 @@
 def packed(w_ref, h_ref, rows, cols, pack):
     count = w_ref.shape[0]
     all_rows = w_ref.shape[1] // 2
-    long = cols + (pack - 1) * LANES
-    tiles = []
+    steps = range(0, count, pack)
     left = jnp.concatenate(
         [
             jnp.concatenate(
                 [w_ref[m + k, base : base + rows] for k in range(pack) for base in (0, all_rows)],
                 0,
             )
-            for m in range(0, count, pack)
+            for m in steps
         ],
         1,
     )
-    col = 0
-    while col < long:
-        width = min(TILE, long - col)
-        tiles.append(dot(left, hankel_tile(h_ref, col, range(0, count, pack), width)))
-        col += width
-    got = jnp.concatenate(tiles, 1)
-    total = got[: 2 * rows, :cols]
-    for k in range(1, pack):
-        total = total + got[2 * rows * k : 2 * rows * (k + 1), k * LANES : k * LANES + cols]
-    return square(total)
+    if pack == 1:
+        return jnp.concatenate(
+            [square(dot(left, hankel_tile(h_ref, col, steps))) for col in range(0, cols, TILE)], 1
+        )
+    done = []
+    for col in range(0, cols, TILE):
+        got = dot(left, hankel_tile(h_ref, col, steps))
+        high = got[2 * rows :]
+        if col > 0:
+            done.append(square(low + jnp.concatenate([rest, high[:, :LANES]], 1)))
+        low, rest = got[: 2 * rows], high[:, LANES:]
+    high = dot(left[2 * rows :], hankel_tile(h_ref, cols, steps, LANES))
+    done.append(square(low + jnp.concatenate([rest, high], 1)))
+    return jnp.concatenate(done, 1)
 
 
 def harmonic_plane(w_ref, all_ref, h_ref, device, unit, num, den):
@@ -149,17 +152,7 @@
     part_rows, part_cols = rows * num // den, all_ref.shape[2] * num // den
     start = device * (part_cols // unit) - taps // 2 // unit
     hankel(bins(all_ref, unit, start, (part_cols + taps) // unit), h_ref)
-    pack = rows // part_rows
-    if pack > 1:
-        return packed(w_ref, h_ref, part_rows, part_cols, min(pack, 2))
-    left = weights(w_ref, range(count), part_rows)
-    return jnp.concatenate(
-        [
-            square(dot(left, hankel_tile(h_ref, col, range(count))))
-            for col in range(0, part_cols, TILE)
-        ],
-        1,
-    )
+    return packed(w_ref, h_ref, part_rows, part_cols, min(2, rows // part_rows))
 
 
 def stretch(plane, num, den):

time: 16.6 us -> 16.5 us (level)
  no operation moved by 1% of the time
where the time goes in v6:
time: 16.5 us; the launch traced here: 16.2 us
  Pallas kernels  7.69 us (47%)
  starting transfers between devices  7.43 us (45%)
  local copies, waits for them, and re-layouts  0.7 us (4%)
  waiting for transfers between devices  0.4 us (2%)
    all_to_all x1, starting transfers between devices, body(): lax.all_to_all(shared, 'freq', split_axis=0, concat_axis=0, tiled=True, a...  7.43 us
    pallas_call x1, Pallas kernels, body(): pl.pallas_call(plane_kernel, out_shape=jax.ShapeDtypeStruct((rows, block)...  4.08 us
    pallas_call x1, Pallas kernels, body(): pl.pallas_call(local_kernel, out_shape=(jax.ShapeDtypeStruct((taps // LAN...  2.94 us
    unnamed x6, local copies, waits for them, and re-layouts  0.7 us
    pallas_call x1, Pallas kernels, body(): pl.pallas_call(share_kernel, out_shape=(jax.ShapeDtypeStruct((owners, 2,...  0.66 us
    all_to_all x1, waiting for transfers between devices, body(): lax.all_to_all(shared, 'freq', split_axis=0, concat_axis=0, tiled=True, a...  0.4 us
  transfers between devices with their start and end apart: 1, of which 1 were waited for; matrix products, arithmetic and copies ran while one was open for 0% of the time, Pallas kernels for 18%

profile of v6, /device:TPU:1, one launch (start us, length us, event | category | flops | bytes accessed | tf_op | source)
XLA Modules:
  0.0 16.2 jit_solution(15953142270439547240)
XLA Ops:
  0.0 0.0 copy-start.1
  0.0 0.0 copy-start.2
  0.0 0.7 %copy-done.1 = bf16[2,2048]{1,0:T(2,128)(2,1)S(1)} copy-done((bf16[2,2048]{1,0:T(2,128)(2,1)S(1)}, bf16[2,2048]{1,0:T(2,128)(2,1)}, u32[]{:S(2)}) %copy-start.1) | copy-done | bytes 8216
  0.7 0.0 copy-done.2
  0.7 0.0 copy-start
  0.7 0.7 %share.1 = (bf16[16,2,2048]{2,1,0:T(2,128)(2,1)}, s32[1,128]{1,0:T(1,128)S(1)}) custom-call(f32[8,128]{1,0:T(8,128)S(1)} %first.1.mark_ref, bf16[2,2048]{1,0:T(2,128)(2,1)S(1)} %copy-done.1, s32[1,128]{1,0:T(1,128)S(1)} %bitcast.1), custom_call_target="tpu_custom_call" | custom-call | flops 4000000000 | bytes 16777216 | tf_op jit(solution)/shard_map/share/pallas_call | solution.py:300
  1.4 7.4 %all-to-all-start = ((bf16[16,2,2048]{2,1,0:T(2,128)(2,1)}), bf16[16,2,2048]{2,1,0:T(2,128)(2,1)S(1)}, u32[]{:S(2)}, u32[]{:S(2)}) async-start(bf16[16,2,2048]{2,1,0:T(2,128)(2,1)} %get-tuple-element.14), calls=%async_computation | async-start | bytes 262144 | tf_op jit(solution)/shard_map/all_to_all | solution.py:312
  8.8 0.0 copy-done
  8.8 2.9 %local.1 = (bf16[8,256,256]{2,1,0:T(8,128)(2,1)S(1)}, bf16[128,1024]{1,0:T(8,128)(2,1)S(1)}, f32[256,1024]{1,0:T(8,128)S(1)}) custom-call(s32[1,128]{1,0:T(1,128)S(1)} %get-tuple-element.10.index_ref, bf16[2,256,1024]{2,1,0:T(8,128)(2,1)S(1)} %copy-done, bf16[2,2048]{1,0:T(2,128)(2,1)S(1)} %copy-done.1), custom_call_target="tpu_custom_call" | custom-call | tf_op jit(solution)/shard_map/local/pallas_call | solution.py:320
  11.8 0.4 %all-to-all-done.all_ref = bf16[16,2,2048]{2,1,0:T(2,128)(2,1)S(1)} async-done(((bf16[16,2,2048]{2,1,0:T(2,128)(2,1)}), bf16[16,2,2048]{2,1,0:T(2,128)(2,1)S(1)}, u32[]{:S(2)}, u32[]{:S(2)}) %all-to-all-start) | async-done | bytes 131104 | tf_op jit(solution)/shard_map/all_to_all | solution.py:312
  12.2 4.1 %plane.1 = f32[128,2048]{1,0:T(8,128)} custom-call(bf16[8,256,256]{2,1,0:T(8,128)(2,1)S(1)} %get-tuple-element.11.w_ref, bf16[128,1024]{1,0:T(8,128)(2,1)S(1)} %get-tuple-element.12.inner_ref, f32[256,1024]{1,0:T(8,128)S(1)} %get-tuple-element.13.edge_ref, bf16[16,2,2048]{2,1,0:T(2,128)(2,1)S(1)} %all-to-all-done.all_ref), custom_call_target="tpu_custom_call" | custom-call | tf_op jit(solution)/shard_map/plane/pallas_call | solution.py:333
  (1 shorter events, 0.0 us)
Async XLA Ops:
  0.0 0.7 %copy-start.1 = (bf16[2,2048]{1,0:T(2,128)(2,1)S(1)}, bf16[2,2048]{1,0:T(2,128)(2,1)}, u32[]{:S(2)}) copy-start(bf16[2,2048]{1,0:T(2,128)(2,1)} %own_ref.3) | copy-start | bytes 24580
  0.0 0.7 %copy-start.2 = (s32[128]{0:T(128)S(1)}, s32[128]{0:T(128)}, u32[]{:S(2)}) copy-start(s32[128]{0:T(128)} %param.5) | copy-start | bytes 1540
  0.7 8.1 %copy-start = (bf16[2,256,1024]{2,1,0:T(8,128)(2,1)S(1)}, bf16[2,256,1024]{2,1,0:T(8,128)(2,1)}, u32[]{:S(2)}) copy-start(bf16[2,256,1024]{2,1,0:T(8,128)(2,1)} %bank_ref.1) | copy-start | bytes 3145732
  1.4 10.8 %all-to-all-start = ((bf16[16,2,2048]{2,1,0:T(2,128)(2,1)}), bf16[16,2,2048]{2,1,0:T(2,128)(2,1)S(1)}, u32[]{:S(2)}, u32[]{:S(2)}) async-start(bf16[16,2,2048]{2,1,0:T(2,128)(2,1)} %get-tuple-element.14), calls=%async_computation | async-start | bytes 262144 | tf_op jit(solution)/shard_map/all_to_all | solution.py:312

commit v7 on v6

--- a/solution.py
+++ b/solution.py
@@ -10,6 +10,7 @@
 LANES = 128
 TILE = 256
 HARMONICS = ((3, 4), (1, 2), (1, 4))
+HELD = HARMONICS[:1]
 F32 = jnp.float32
 BF16 = jnp.bfloat16
 VMEM = pl.BlockSpec(memory_space=pltpu.VMEM)
@@ -50,13 +51,17 @@
     )
 
 
-def weights(w_ref, steps, rows=None):
-    all_rows = w_ref.shape[1] // 2
-    if rows is None:
-        return jnp.concatenate([w_ref[m] for m in steps], 1)
+def half_step(w_ref, m, part, rows):
+    all_rows = w_ref.shape[1] // 3
+    picked = ((0, 2), (1, 0))[part]
+    return jnp.concatenate([w_ref[m, k * all_rows : k * all_rows + rows, :] for k in picked], 1)
+
+
+def weights(w_ref, steps):
+    rows = w_ref.shape[1] // 3
     return jnp.concatenate(
         [
-            jnp.concatenate([w_ref[m, :rows], w_ref[m, all_rows : all_rows + rows]], 0)
+            jnp.concatenate([half_step(w_ref, m, part, rows) for part in (0, 1)], 0)
             for m in steps
         ],
         1,
@@ -73,7 +78,9 @@
     index_out_ref[...] = index_ref[...]
 
 
-def local_kernel(index_ref, bank_ref, own_ref, w_ref, inner_ref, edge_ref, h_ref):
+def local_kernel(
+    index_ref, bank_ref, own_ref, w_ref, inner_ref, edge_ref, picks_ref, expand_ref, h_ref
+):
     rows = index_ref.shape[1]
     bank = bank_ref.shape[1]
     taps = bank_ref.shape[2]
@@ -97,10 +104,10 @@
                 )
             )
         re, im = part
-        w_ref[m, :rows, :LANES] = re.astype(BF16)
-        w_ref[m, :rows, LANES:] = (-im).astype(BF16)
-        w_ref[m, rows:, :LANES] = im.astype(BF16)
-        w_ref[m, rows:, LANES:] = re.astype(BF16)
+        w_ref[m, :rows] = re.astype(BF16)
+        w_ref[m, rows : 2 * rows] = im.astype(BF16)
+        w_ref[m, 2 * rows :] = (-im).astype(BF16)
+    write_constants(picks_ref, expand_ref, block)
     for col in range(0, block, TILE):
         steps = [
             m
@@ -117,12 +124,12 @@
 
 def packed(w_ref, h_ref, rows, cols, pack):
     count = w_ref.shape[0]
-    all_rows = w_ref.shape[1] // 2
+    all_rows = w_ref.shape[1] // 3
     steps = range(0, count, pack)
     left = jnp.concatenate(
         [
             jnp.concatenate(
-                [w_ref[m + k, base : base + rows] for k in range(pack) for base in (0, all_rows)],
+                [half_step(w_ref, m + k, part, rows) for k in range(pack) for part in (0, 1)],
                 0,
             )
             for m in steps
@@ -147,7 +154,7 @@
 
 def harmonic_plane(w_ref, all_ref, h_ref, device, unit, num, den):
     count = w_ref.shape[0]
-    rows = w_ref.shape[1] // 2
+    rows = w_ref.shape[1] // 3
     taps = count * LANES
     part_rows, part_cols = rows * num // den, all_ref.shape[2] * num // den
     start = device * (part_cols // unit) - taps // 2 // unit
@@ -155,23 +162,55 @@
     return packed(w_ref, h_ref, part_rows, part_cols, min(2, rows // part_rows))
 
 
-def stretch(plane, num, den):
-    part_rows, part_cols = plane.shape
+def stretch_plan(part_cols, num, den):
     tiles = part_cols * den // num // TILE
     starts = [j * TILE * num // den for j in range(tiles)]
-    wide = -(-(max(start % LANES for start in starts) + TILE * num // den) // LANES) * LANES
+    offsets = sorted({start % LANES for start in starts})
+    wide = -(-(max(offsets) + TILE * num // den) // LANES) * LANES
+    return starts, offsets, wide
+
+
+def expands(block):
+    got = {}
+    base = 0
+    for num, den in HELD:
+        _, offsets, wide = stretch_plan(block * num // den, num, den)
+        for offset in offsets[:1]:
+            got[num, den, offset] = slice(base, base + wide)
+            base += wide
+    return got
+
+
+def one_hot(wide, offset, num, den):
+    shape = (wide, TILE)
+    return (iota(shape, 1) * num // den + offset == iota(shape, 0)).astype(BF16)
+
+
+def write_constants(picks_ref, expand_ref, block):
+    rows = picks_ref.shape[0]
+    parts = []
+    for num, den in HARMONICS:
+        shape = (rows, rows * num // den)
+        parts.append((iota(shape, 0) * num // den == iota(shape, 1)).astype(BF16))
+    picks_ref[...] = jnp.concatenate(parts, 1)
+    for (num, den, offset), at in expands(block).items():
+        expand_ref[at, :] = one_hot(at.stop - at.start, offset, num, den)
+
+
+def stretch(plane, expand_ref, block, num, den):
+    part_rows, part_cols = plane.shape
+    starts, offsets, wide = stretch_plan(part_cols, num, den)
     done = {}
-    for offset in sorted({start % LANES for start in starts}):
-        members = [j for j in range(tiles) if starts[j] % LANES == offset]
-        expand = (
-            iota((wide, TILE), 1) * num // den + offset == iota((wide, TILE), 0)
-        ).astype(BF16)
+    for offset in offsets:
+        members = [j for j, start in enumerate(starts) if start % LANES == offset]
         bases = [starts[j] - offset for j in members]
         stacked = jnp.concatenate([plane[:, base : base + wide] for base in bases], 0)
-        spread = dot(stacked, expand).astype(BF16)
-        for n, j in enumerate(members):
-            done[j] = spread[n * part_rows : (n + 1) * part_rows]
-    return jnp.concatenate([done[j] for j in range(tiles)], 1)
+        at = expands(block).get((num, den, offset))
+        matrix = one_hot(wide, offset, num, den) if at is None else expand_ref[at, :]
+        spread = dot(stacked, matrix).astype(BF16)
+        for k, j in enumerate(members):
+            done[j] = spread[k * part_rows : (k + 1) * part_rows]
+    return jnp.concatenate([done[j] for j in range(len(starts))], 1)
 
 
 def group_order(owners):
@@ -225,18 +264,9 @@
     return jnp.concatenate(edges[:middle] + [inner_ref[...]] + edges[middle:], 1)
 
 
-def write_sum(own, pieces, out_ref, buffer_ref, sems):
-    rows, block = buffer_ref.shape
-    picks = jnp.concatenate(
-        [
-            (
-                iota((rows, rows * num // den), 0) * num // den
-                == iota((rows, rows * num // den), 1)
-            ).astype(BF16)
-            for num, den in HARMONICS
-        ],
-        1,
-    )
+def write_sum(own, pieces, picks_ref, out_ref, buffer_ref, sems):
+    block = buffer_ref.shape[1]
+    picks = picks_ref[...]
     chunks = sems.shape[0]
     width = block // chunks
     copies = []
@@ -252,10 +282,10 @@
 
 
 def plane_kernel(
-    w_ref, inner_ref, edge_ref, all_ref, out_ref, side_ref, buffer_ref, sems, *h_refs
+    w_ref, inner_ref, edge_ref, picks_ref, expand_ref, all_ref, out_ref, side_ref, buffer_ref, sems, *h_refs
 ):
     block = all_ref.shape[2]
-    rows = w_ref.shape[1] // 2
+    rows = w_ref.shape[1] // 3
     half = w_ref.shape[0] * LANES // 2
     device = lax.axis_index("freq")
     unit = math.gcd(half, *(block * num // den for num, den in HARMONICS))
@@ -266,18 +296,21 @@
             harmonic_plane(w_ref, all_ref, h_ref, device, unit, num, den)
             for (num, den), h_ref in zip(HARMONICS, h_refs)
         ]
-        pieces = [stretch(plane, num, den) for plane, (num, den) in zip(planes, HARMONICS)]
+        pieces = [
+            stretch(plane, expand_ref, block, num, den)
+            for plane, (num, den) in zip(planes, HARMONICS)
+        ]
         own = own_plane(w_ref, inner_ref, edge_ref, all_ref, side_ref, device, unit)
-        write_sum(own, pieces, out_ref, buffer_ref, sems)
+        write_sum(own, pieces, picks_ref, out_ref, buffer_ref, sems)
 
     @pl.when(device == 0)
     def _():
         own = own_plane(w_ref, inner_ref, edge_ref, all_ref, side_ref, device, unit)
         pieces = [
-            stretch(own[: rows * num // den, : block * num // den], num, den)
+            stretch(own[: rows * num // den, : block * num // den], expand_ref, block, num, den)
             for num, den in HARMONICS
         ]
-        write_sum(own, pieces, out_ref, buffer_ref, sems)
+        write_sum(own, pieces, picks_ref, out_ref, buffer_ref, sems)
 
 
 def body(spectrum, template_bank, template_index):
@@ -286,6 +319,7 @@
     rows = template_index.shape[0]
     taps = template_bank.shape[2]
     half = taps // 2
+    matrix_rows = max(at.stop for at in expands(block).values())
     hankels = [
         pltpu.VMEM((2 * LANES, block * num // den + taps - LANES), BF16) for num, den in HARMONICS
     ]
@@ -317,15 +351,17 @@
         tiled=True,
         axis_index_groups=[list(group_order(owners))],
     )
-    w, inner, edge = pl.pallas_call(
+    w, inner, edge, picks, expand = pl.pallas_call(
         local_kernel,
         out_shape=(
-            jax.ShapeDtypeStruct((taps // LANES, 2 * rows, 2 * LANES), BF16),
+            jax.ShapeDtypeStruct((taps // LANES, 3 * rows, LANES), BF16),
             jax.ShapeDtypeStruct((rows, block - 2 * half), BF16),
             jax.ShapeDtypeStruct((2 * rows, 2 * half), F32),
+            jax.ShapeDtypeStruct((rows, sum(rows * num // den for num, den in HARMONICS)), BF16),
+            jax.ShapeDtypeStruct((matrix_rows, TILE), BF16),
         ),
         in_specs=[VMEM] * 3,
-        out_specs=(VMEM,) * 3,
+        out_specs=(VMEM,) * 5,
         scratch_shapes=[pltpu.VMEM((2 * LANES, block + taps - LANES), BF16)],
         compiler_params=pltpu.CompilerParams(vmem_limit_bytes=24 << 20),
         name="local",
@@ -333,7 +369,7 @@
     return pl.pallas_call(
         plane_kernel,
         out_shape=jax.ShapeDtypeStruct((rows, block), F32),
-        in_specs=[VMEM] * 4,
+        in_specs=[VMEM] * 6,
         out_specs=ANY,
         scratch_shapes=[
             pltpu.VMEM((2, 2 * LANES, half + TILE), BF16),
@@ -343,7 +379,7 @@
         + hankels,
         compiler_params=pltpu.CompilerParams(vmem_limit_bytes=32 << 20),
         name="plane",
-    )(w, inner, edge, everything)
+    )(w, inner, edge, picks, expand, everything)
 
 
 def solution(mesh):

time: 16.5 us -> 16.5 us (level)
  no operation moved by 1% of the time
where the time goes in v7:
time: 16.5 us; the launch traced here: 16.1 us
  Pallas kernels  7.62 us (46%)
  starting transfers between devices  7.43 us (45%)
  local copies, waits for them, and re-layouts  0.7 us (4%)
  waiting for transfers between devices  0.4 us (2%)
    all_to_all x1, starting transfers between devices, body(): lax.all_to_all(shared, 'freq', split_axis=0, concat_axis=0, tiled=True, a...  7.43 us
    pallas_call x1, Pallas kernels, body(): pl.pallas_call(plane_kernel, out_shape=jax.ShapeDtypeStruct((rows, block)...  4 us
    pallas_call x1, Pallas kernels, body(): pl.pallas_call(local_kernel, out_shape=(jax.ShapeDtypeStruct((taps // LAN...  2.95 us
    unnamed x6, local copies, waits for them, and re-layouts  0.7 us
    pallas_call x1, Pallas kernels, body(): pl.pallas_call(share_kernel, out_shape=(jax.ShapeDtypeStruct((owners, 2,...  0.66 us
    all_to_all x1, waiting for transfers between devices, body(): lax.all_to_all(shared, 'freq', split_axis=0, concat_axis=0, tiled=True, a...  0.4 us
  transfers between devices with their start and end apart: 1, of which 1 were waited for; matrix products, arithmetic and copies ran while one was open for 0% of the time, Pallas kernels for 18%

profile of v7, /device:TPU:1, one launch (start us, length us, event | category | flops | bytes accessed | tf_op | source)
XLA Modules:
  0.0 16.1 jit_solution(2557769460996060645)
XLA Ops:
  0.0 0.0 copy-start.1
  0.0 0.0 copy-start.2
  0.0 0.7 %copy-done.1 = bf16[2,2048]{1,0:T(2,128)(2,1)S(1)} copy-done((bf16[2,2048]{1,0:T(2,128)(2,1)S(1)}, bf16[2,2048]{1,0:T(2,128)(2,1)}, u32[]{:S(2)}) %copy-start.1) | copy-done | bytes 8216
  0.7 0.0 copy-done.2
  0.7 0.0 copy-start
  0.7 0.7 %share.1 = (bf16[16,2,2048]{2,1,0:T(2,128)(2,1)}, s32[1,128]{1,0:T(1,128)S(1)}) custom-call(f32[8,128]{1,0:T(8,128)S(1)} %first.1.mark_ref, bf16[2,2048]{1,0:T(2,128)(2,1)S(1)} %copy-done.1, s32[1,128]{1,0:T(1,128)S(1)} %bitcast.1), custom_call_target="tpu_custom_call" | custom-call | flops 4000000000 | bytes 16777216 | tf_op jit(solution)/shard_map/share/pallas_call | solution.py:334
  1.4 7.4 %all-to-all-start = ((bf16[16,2,2048]{2,1,0:T(2,128)(2,1)}), bf16[16,2,2048]{2,1,0:T(2,128)(2,1)S(1)}, u32[]{:S(2)}, u32[]{:S(2)}) async-start(bf16[16,2,2048]{2,1,0:T(2,128)(2,1)} %get-tuple-element.18), calls=%async_computation | async-start | bytes 262144 | tf_op jit(solution)/shard_map/all_to_all | solution.py:346
  8.8 0.0 copy-done
  8.8 3.0 %local.1 = (bf16[8,384,128]{2,1,0:T(8,128)(2,1)S(1)}, bf16[128,1024]{1,0:T(8,128)(2,1)S(1)}, f32[256,1024]{1,0:T(8,128)S(1)}, bf16[128,192]{1,0:T(8,128)(2,1)S(1)}, bf16[256,256]{1,0:T(8,128)(2,1)S(1)}) custom-call(s32[1,128]{1,0:T(1,128)S(1)} %get-tuple-element.12.index_ref, bf16[2,256,1024]{2,1,0:T(8,128)(2,1)S(1)} %copy-done, bf16[2,2048]{1,0:T(2,128)(2,1)S(1)} %copy-done.1), custom_call_target="tpu_custom_call" | custom-call | tf_op jit(solution)/shard_map/local/pallas_call | solution.py:354
  11.8 0.4 %all-to-all-done.all_ref = bf16[16,2,2048]{2,1,0:T(2,128)(2,1)S(1)} async-done(((bf16[16,2,2048]{2,1,0:T(2,128)(2,1)}), bf16[16,2,2048]{2,1,0:T(2,128)(2,1)S(1)}, u32[]{:S(2)}, u32[]{:S(2)}) %all-to-all-start) | async-done | bytes 131104 | tf_op jit(solution)/shard_map/all_to_all | solution.py:346
  12.2 4.0 %plane.1 = f32[128,2048]{1,0:T(8,128)} custom-call(bf16[8,384,128]{2,1,0:T(8,128)(2,1)S(1)} %get-tuple-element.13.w_ref, bf16[128,1024]{1,0:T(8,128)(2,1)S(1)} %get-tuple-element.14.inner_ref, f32[256,1024]{1,0:T(8,128)S(1)} %get-tuple-element.15.edge_ref, bf16[128,192]{1,0:T(8,128)(2,1)S(1)} %get-tuple-element.16.picks_ref, ...), custom_call_target="tpu_custom_call" | custom-call | tf_op jit(solution)/shard_map/plane/pallas_call | solution.py:369
  (1 shorter events, 0.0 us)
Async XLA Ops:
  0.0 0.7 %copy-start.1 = (bf16[2,2048]{1,0:T(2,128)(2,1)S(1)}, bf16[2,2048]{1,0:T(2,128)(2,1)}, u32[]{:S(2)}) copy-start(bf16[2,2048]{1,0:T(2,128)(2,1)} %own_ref.3) | copy-start | bytes 24580
  0.0 0.7 %copy-start.2 = (s32[128]{0:T(128)S(1)}, s32[128]{0:T(128)}, u32[]{:S(2)}) copy-start(s32[128]{0:T(128)} %param.5) | copy-start | bytes 1540
  0.7 8.1 %copy-start = (bf16[2,256,1024]{2,1,0:T(8,128)(2,1)S(1)}, bf16[2,256,1024]{2,1,0:T(8,128)(2,1)}, u32[]{:S(2)}) copy-start(bf16[2,256,1024]{2,1,0:T(8,128)(2,1)} %bank_ref.1) | copy-start | bytes 3145732
  1.4 10.8 %all-to-all-start = ((bf16[16,2,2048]{2,1,0:T(2,128)(2,1)}), bf16[16,2,2048]{2,1,0:T(2,128)(2,1)S(1)}, u32[]{:S(2)}, u32[]{:S(2)}) async-start(bf16[16,2,2048]{2,1,0:T(2,128)(2,1)} %get-tuple-element.18), calls=%async_computation | async-start | bytes 262144 | tf_op jit(solution)/shard_map/all_to_all | solution.py:346

commit v8 on v7

--- a/solution.py
+++ b/solution.py
@@ -10,7 +10,7 @@
 LANES = 128
 TILE = 256
 HARMONICS = ((3, 4), (1, 2), (1, 4))
-HELD = HARMONICS[:1]
+HELD = HARMONICS[:2]
 F32 = jnp.float32
 BF16 = jnp.bfloat16
 VMEM = pl.BlockSpec(memory_space=pltpu.VMEM)

time: 16.5 us -> 16.5 us (level)
  no operation moved by 1% of the time
where the time goes in v8:
time: 16.5 us; the launch traced here: 16.1 us
  Pallas kernels  7.61 us (46%)
  starting transfers between devices  7.43 us (45%)
  local copies, waits for them, and re-layouts  0.7 us (4%)
  waiting for transfers between devices  0.4 us (2%)
    all_to_all x1, starting transfers between devices, body(): lax.all_to_all(shared, 'freq', split_axis=0, concat_axis=0, tiled=True, a...  7.43 us
    pallas_call x1, Pallas kernels, body(): pl.pallas_call(plane_kernel, out_shape=jax.ShapeDtypeStruct((rows, block)...  4 us
    pallas_call x1, Pallas kernels, body(): pl.pallas_call(local_kernel, out_shape=(jax.ShapeDtypeStruct((taps // LAN...  2.95 us
    unnamed x6, local copies, waits for them, and re-layouts  0.7 us
    pallas_call x1, Pallas kernels, body(): pl.pallas_call(share_kernel, out_shape=(jax.ShapeDtypeStruct((owners, 2,...  0.66 us
    all_to_all x1, waiting for transfers between devices, body(): lax.all_to_all(shared, 'freq', split_axis=0, concat_axis=0, tiled=True, a...  0.4 us
  transfers between devices with their start and end apart: 1, of which 1 were waited for; matrix products, arithmetic and copies ran while one was open for 0% of the time, Pallas kernels for 18%

profile of v8, /device:TPU:1, one launch (start us, length us, event | category | flops | bytes accessed | tf_op | source)
XLA Modules:
  0.0 16.1 jit_solution(6131115749469549866)
XLA Ops:
  0.0 0.0 copy-start.1
  0.0 0.0 copy-start.2
  0.0 0.7 %copy-done.1 = bf16[2,2048]{1,0:T(2,128)(2,1)S(1)} copy-done((bf16[2,2048]{1,0:T(2,128)(2,1)S(1)}, bf16[2,2048]{1,0:T(2,128)(2,1)}, u32[]{:S(2)}) %copy-start.1) | copy-done | bytes 8216
  0.7 0.0 copy-done.2
  0.7 0.0 copy-start
  0.7 0.7 %share.1 = (bf16[16,2,2048]{2,1,0:T(2,128)(2,1)}, s32[1,128]{1,0:T(1,128)S(1)}) custom-call(f32[8,128]{1,0:T(8,128)S(1)} %first.1.mark_ref, bf16[2,2048]{1,0:T(2,128)(2,1)S(1)} %copy-done.1, s32[1,128]{1,0:T(1,128)S(1)} %bitcast.1), custom_call_target="tpu_custom_call" | custom-call | flops 4000000000 | bytes 16777216 | tf_op jit(solution)/shard_map/share/pallas_call | solution.py:334
  1.4 7.4 %all-to-all-start = ((bf16[16,2,2048]{2,1,0:T(2,128)(2,1)}), bf16[16,2,2048]{2,1,0:T(2,128)(2,1)S(1)}, u32[]{:S(2)}, u32[]{:S(2)}) async-start(bf16[16,2,2048]{2,1,0:T(2,128)(2,1)} %get-tuple-element.18), calls=%async_computation | async-start | bytes 262144 | tf_op jit(solution)/shard_map/all_to_all | solution.py:346
  8.8 0.0 copy-done
  8.8 3.0 %local.1 = (bf16[8,384,128]{2,1,0:T(8,128)(2,1)S(1)}, bf16[128,1024]{1,0:T(8,128)(2,1)S(1)}, f32[256,1024]{1,0:T(8,128)S(1)}, bf16[128,192]{1,0:T(8,128)(2,1)S(1)}, bf16[384,256]{1,0:T(8,128)(2,1)S(1)}) custom-call(s32[1,128]{1,0:T(1,128)S(1)} %get-tuple-element.12.index_ref, bf16[2,256,1024]{2,1,0:T(8,128)(2,1)S(1)} %copy-done, bf16[2,2048]{1,0:T(2,128)(2,1)S(1)} %copy-done.1), custom_call_target="tpu_custom_call" | custom-call | tf_op jit(solution)/shard_map/local/pallas_call | solution.py:354
  11.8 0.4 %all-to-all-done.all_ref = bf16[16,2,2048]{2,1,0:T(2,128)(2,1)S(1)} async-done(((bf16[16,2,2048]{2,1,0:T(2,128)(2,1)}), bf16[16,2,2048]{2,1,0:T(2,128)(2,1)S(1)}, u32[]{:S(2)}, u32[]{:S(2)}) %all-to-all-start) | async-done | bytes 131104 | tf_op jit(solution)/shard_map/all_to_all | solution.py:346
  12.2 4.0 %plane.1 = f32[128,2048]{1,0:T(8,128)} custom-call(bf16[8,384,128]{2,1,0:T(8,128)(2,1)S(1)} %get-tuple-element.13.w_ref, bf16[128,1024]{1,0:T(8,128)(2,1)S(1)} %get-tuple-element.14.inner_ref, f32[256,1024]{1,0:T(8,128)S(1)} %get-tuple-element.15.edge_ref, bf16[128,192]{1,0:T(8,128)(2,1)S(1)} %get-tuple-element.16.picks_ref, ...), custom_call_target="tpu_custom_call" | custom-call | tf_op jit(solution)/shard_map/plane/pallas_call | solution.py:369
  (1 shorter events, 0.0 us)
Async XLA Ops:
  0.0 0.7 %copy-start.1 = (bf16[2,2048]{1,0:T(2,128)(2,1)S(1)}, bf16[2,2048]{1,0:T(2,128)(2,1)}, u32[]{:S(2)}) copy-start(bf16[2,2048]{1,0:T(2,128)(2,1)} %own_ref.3) | copy-start | bytes 24580
  0.0 0.7 %copy-start.2 = (s32[128]{0:T(128)S(1)}, s32[128]{0:T(128)}, u32[]{:S(2)}) copy-start(s32[128]{0:T(128)} %param.5) | copy-start | bytes 1540
  0.7 8.1 %copy-start = (bf16[2,256,1024]{2,1,0:T(8,128)(2,1)S(1)}, bf16[2,256,1024]{2,1,0:T(8,128)(2,1)}, u32[]{:S(2)}) copy-start(bf16[2,256,1024]{2,1,0:T(8,128)(2,1)} %bank_ref.1) | copy-start | bytes 3145732
  1.4 10.8 %all-to-all-start = ((bf16[16,2,2048]{2,1,0:T(2,128)(2,1)}), bf16[16,2,2048]{2,1,0:T(2,128)(2,1)S(1)}, u32[]{:S(2)}, u32[]{:S(2)}) async-start(bf16[16,2,2048]{2,1,0:T(2,128)(2,1)} %get-tuple-element.18), calls=%async_computation | async-start | bytes 262144 | tf_op jit(solution)/shard_map/all_to_all | solution.py:346
